TPU v7x, 32 devices: a whole 2x2x4 slice. The times are simulated.
32 devices in a mesh: dp: 16 (over z, y, core), tensor: 2 (over x).
Axes of the slice: x: 2, y: 2, z: 4, core: 2. Of those that a mesh axis runs over, the one named last changes fastest.
Arguments:
- tokens: bfloat16 [8192, 768], P('dp'), may hold values from -6 to 6
- lengths: int32 [16], P('dp'), may hold values from 128 to 512, as said below
- positions: int32 [16, 76], P('dp'), may hold values from 0 to 512, as said below
- swap_ids: int32 [16, 76], P('dp'), may hold values from 0 to 255
- swap_rows: bfloat16 [256, 768], replicated, may hold values from -6 to 6
- w_query: bfloat16 [768, 768], P(None, 'tensor'), may hold values from -0.21875 to 0.21875
- b_query: bfloat16 [768], P('tensor'), may hold values from -3 to 3
- w_key: bfloat16 [768, 768], P(None, 'tensor'), may hold values from -0.21875 to 0.21875
- w_value: bfloat16 [768, 768], P(None, 'tensor'), may hold values from -0.21875 to 0.21875
- b_value: bfloat16 [768], P('tensor'), may hold values from -3 to 3
- w_out: bfloat16 [768, 768], P('tensor'), may hold values from -1.25 to 1.25
- b_out: bfloat16 [768], replicated, may hold values from -3 to 3
- first_gain: bfloat16 [768], replicated, may hold values from 0.5 to 1.5
- first_shift: bfloat16 [768], replicated, may hold values from -2.5 to 2.5
- w_up: bfloat16 [768, 3072], P(None, 'tensor'), may hold values from -0.21875 to 0.21875
- b_up: bfloat16 [3072], P('tensor'), may hold values from -3 to 3
- w_down: bfloat16 [3072, 768], P('tensor'), may hold values from -0.109375 to 0.109375
- b_down: bfloat16 [768], replicated, may hold values from -3 to 3
- second_gain: bfloat16 [768], replicated, may hold values from 0.5 to 1.5
- second_shift: bfloat16 [768], replicated, may hold values from -2.5 to 2.5
- cotangent: bfloat16 [8192, 768], P('dp'), may hold values from -6 to 6
Outputs:
- layer_out: bfloat16 [8192, 768], P('dp')
- grad_tokens: float32 [8192, 768], P('dp')
- grad_swap_rows: float32 [256, 768], replicated
- grad_w_query: float32 [768, 768], P(None, 'tensor')
- grad_b_query: float32 [768], P('tensor')
- grad_w_key: float32 [768, 768], P(None, 'tensor')
- grad_w_value: float32 [768, 768], P(None, 'tensor')
- grad_b_value: float32 [768], P('tensor')
- grad_w_out: float32 [768, 768], P('tensor')
- grad_b_out: float32 [768], replicated
- grad_first_gain: float32 [768], replicated
- grad_first_shift: float32 [768], replicated
- grad_w_up: float32 [768, 3072], P(None, 'tensor')
- grad_b_up: float32 [3072], P('tensor')
- grad_w_down: float32 [3072, 768], P('tensor')
- grad_b_down: float32 [768], replicated
- grad_second_gain: float32 [768], replicated
- grad_second_shift: float32 [768], replicated
Inputs may be any that keep to these rules, and one draw needn't show every extreme that they name: `lengths`: at least one page has exactly 512 valid tokens and one has exactly 128. `positions`: slot s of page p holds a position below lengths[p], distinct within the page, when s < lengths[p] * 3 // 20, and 512 (no replacement) otherwise. `swap_ids`: read only where the slot's position is below 512.
All inputs are finite; a program needn't handle non-finite values.
Results may differ from a plain program's by a relative error of at most 0.013.
The roundings to bfloat16 on the way count: a program that leaves them out, or rounds other values in their place, can miss the bound.
Values sent between devices are 32-bit elements; how exact they have to be, the bound alone decides.
A program may use at most 128 MiB of HBM per device.

v0:
```python
import jax
import jax.numpy as jnp
from jax import lax
from jax.sharding import PartitionSpec as P

HEAD_DIM = 64


norm_eps = 1e-12
mask_fill = -1000000000.0
half_root = 0.7071067811865476
gauss_norm = 0.3989422804014327


def to_bf(value):
    return value.astype(jnp.bfloat16)


def product(left, right):
    return jnp.dot(left, right, preferred_element_type=jnp.float32)


def left_product(left, right):
    return lax.dot_general(
        left, right, (((0,), (0,)), ((), ())), preferred_element_type=jnp.float32
    )


def right_product(left, right):
    return lax.dot_general(
        left, right, (((1,), (1,)), ((), ())), preferred_element_type=jnp.float32
    )


def layer_norm(hidden, norm_gain, norm_shift):
    row_mean = jnp.mean(hidden, axis=-1, keepdims=True)
    centred = hidden - row_mean
    inv_std = lax.rsqrt(jnp.mean(centred * centred, axis=-1, keepdims=True) + norm_eps)
    normed = centred * inv_std
    return (normed * norm_gain + norm_shift, normed, inv_std)


def norm_back(upstream, normed, inv_std, norm_gain):
    scaled = upstream * norm_gain
    return inv_std * (
        scaled
        - jnp.mean(scaled, axis=-1, keepdims=True)
        - normed * jnp.mean(scaled * normed, axis=-1, keepdims=True)
    )


def gelu_slope(pre_act):
    return (
        0.5 * (1.0 + lax.erf(pre_act * half_root))
        + pre_act * jnp.exp(-0.5 * pre_act * pre_act) * gauss_norm
    )


def page_scores(queries, keys_page, length):
    key_bias = jnp.where(jnp.arange(keys_page.shape[0]) < length, 0.0, mask_fill).astype(
        jnp.float32
    )
    scores = jnp.einsum("qhe,khe->hqk", queries, keys_page, preferred_element_type=jnp.float32)
    return scores + key_bias[None, None, :]


def page_forward(page_block):
    queries, keys_page, values_page, length = page_block
    scores = page_scores(queries, keys_page, length)
    row_max = jnp.max(scores, axis=-1, keepdims=True)
    exponent = jnp.exp(scores - row_max)
    row_total = jnp.sum(exponent, axis=-1, keepdims=True)
    probs_low = to_bf(exponent / row_total)
    mixed_page = jnp.einsum(
        "hqk,khe->qhe", probs_low, values_page, preferred_element_type=jnp.float32
    )
    return (mixed_page, (row_max + jnp.log(row_total))[:, :, 0])


def page_backward(page_block):
    queries, keys_page, values_page, length, log_total, grad_mixed = page_block
    scores = page_scores(queries, keys_page, length)
    probs = jnp.exp(scores - log_total[:, :, None])
    grad_probs = jnp.einsum(
        "qhe,khe->hqk", grad_mixed, values_page, preferred_element_type=jnp.float32
    )
    grad_scores = to_bf(probs * (grad_probs - jnp.sum(probs * grad_probs, axis=-1, keepdims=True)))
    grad_queries = to_bf(
        jnp.einsum("hqk,khe->qhe", grad_scores, keys_page, preferred_element_type=jnp.float32)
    )
    grad_keys = to_bf(
        jnp.einsum("hqk,qhe->khe", grad_scores, queries, preferred_element_type=jnp.float32)
    )
    grad_values = to_bf(
        jnp.einsum("hqk,qhe->khe", to_bf(probs), grad_mixed, preferred_element_type=jnp.float32)
    )
    return (grad_queries, grad_keys, grad_values)


def split_pages(flat_part, page_count):
    return flat_part.reshape(page_count, -1, flat_part.shape[1] // HEAD_DIM, HEAD_DIM)


def forward(inputs, lengths, weights_all):
    (
        w_query,
        b_query,
        w_key,
        w_value,
        b_value,
        w_out,
        b_out,
        first_gain,
        first_shift,
        w_up,
        b_up,
        w_down,
        b_down,
        second_gain,
        second_shift,
    ) = weights_all
    page_count = lengths.shape[0]
    row_count = inputs.shape[0]
    query_scale = HEAD_DIM ** (-0.5)
    queries = to_bf((product(inputs, w_query) + b_query) * query_scale)
    keys_all = to_bf(product(inputs, w_key))
    values_all = to_bf(product(inputs, w_value) + b_value)
    mixed_heads, log_total = lax.map(
        page_forward,
        (
            split_pages(queries, page_count),
            split_pages(keys_all, page_count),
            split_pages(values_all, page_count),
            lengths,
        ),
    )
    mixed_heads = to_bf(mixed_heads.reshape(row_count, -1))
    branch = lax.psum(product(mixed_heads, w_out), "tensor") + b_out
    first_out, first_normed, first_inv = layer_norm(
        inputs.astype(jnp.float32) + branch, first_gain, first_shift
    )
    first_low = to_bf(first_out)
    up_pre = product(first_low, w_up) + b_up
    up_act = to_bf(jax.nn.gelu(up_pre, approximate=False))
    down_out = lax.psum(product(up_act, w_down), "tensor") + b_down
    result, second_normed, second_inv = layer_norm(first_out + down_out, second_gain, second_shift)
    kept_values = (
        queries,
        keys_all,
        values_all,
        mixed_heads,
        log_total,
        first_normed,
        first_inv,
        first_low,
        up_pre,
        up_act,
        second_normed,
        second_inv,
    )
    return (result, kept_values)


def local(
    tokens,
    lengths,
    positions,
    swap_ids,
    swap_rows,
    w_query,
    b_query,
    w_key,
    w_value,
    b_value,
    w_out,
    b_out,
    first_gain,
    first_shift,
    w_up,
    b_up,
    w_down,
    b_down,
    second_gain,
    second_shift,
    cotangent,
):
    page_count = lengths.shape[0]
    row_count, model_width = tokens.shape
    page_rows = row_count // page_count
    hit_table = positions[:, None, :] == jnp.arange(page_rows)[None, :, None]
    pick_table = swap_ids[:, :, None] == jnp.arange(swap_rows.shape[0])[None, None, :]
    chosen = to_bf(
        jnp.einsum(
            "psr,rd->psd",
            pick_table.astype(jnp.bfloat16),
            swap_rows,
            preferred_element_type=jnp.float32,
        )
    )
    placed = jnp.einsum(
        "pts,psd->ptd", hit_table.astype(jnp.bfloat16), chosen, preferred_element_type=jnp.float32
    )
    replaced = jnp.any(hit_table, axis=-1)[:, :, None]
    inputs = jnp.where(replaced, to_bf(placed), tokens.reshape(page_count, page_rows, model_width))
    inputs = inputs.reshape(row_count, model_width)
    weights_all = (
        w_query,
        b_query,
        w_key,
        w_value,
        b_value,
        w_out,
        b_out,
        first_gain,
        first_shift,
        w_up,
        b_up,
        w_down,
        b_down,
        second_gain,
        second_shift,
    )
    result, kept_values = forward(inputs, lengths, weights_all)
    inputs_again, unused = lax.optimization_barrier((inputs, result))
    unused, kept_values = forward(inputs_again, lengths, weights_all)
    (
        queries,
        keys_all,
        values_all,
        mixed_heads,
        log_total,
        first_normed,
        first_inv,
        first_low,
        up_pre,
        up_act,
        second_normed,
        second_inv,
    ) = kept_values
    grad_out = cotangent.astype(jnp.float32)
    grad_second_gain = jnp.sum(grad_out * second_normed, axis=0)
    grad_second_shift = jnp.sum(grad_out, axis=0)
    grad_second = norm_back(grad_out, second_normed, second_inv, second_gain)
    grad_down = to_bf(grad_second)
    grad_b_down = jnp.sum(grad_down.astype(jnp.float32), axis=0)
    grad_w_down = left_product(up_act, grad_down)
    grad_pre = to_bf(right_product(grad_down, w_down) * gelu_slope(up_pre))
    grad_b_up = jnp.sum(grad_pre.astype(jnp.float32), axis=0)
    grad_w_up = left_product(first_low, grad_pre)
    grad_first = grad_second + lax.psum(right_product(grad_pre, w_up), "tensor")
    grad_first_gain = jnp.sum(grad_first * first_normed, axis=0)
    grad_first_shift = jnp.sum(grad_first, axis=0)
    grad_resid = norm_back(grad_first, first_normed, first_inv, first_gain)
    grad_branch = to_bf(grad_resid)
    grad_b_out = jnp.sum(grad_branch.astype(jnp.float32), axis=0)
    grad_w_out = left_product(mixed_heads, grad_branch)
    grad_mixed = to_bf(right_product(grad_branch, w_out))
    grad_queries, grad_keys, grad_values = lax.map(
        page_backward,
        (
            split_pages(queries, page_count),
            split_pages(keys_all, page_count),
            split_pages(values_all, page_count),
            lengths,
            log_total,
            split_pages(grad_mixed, page_count),
        ),
    )
    grad_queries = grad_queries.reshape(row_count, -1) * HEAD_DIM ** (-0.5)
    grad_keys = grad_keys.reshape(row_count, -1)
    grad_values = grad_values.reshape(row_count, -1)
    grad_w_query = left_product(inputs, grad_queries)
    grad_b_query = jnp.sum(grad_queries.astype(jnp.float32), axis=0)
    grad_w_key = left_product(inputs, grad_keys)
    grad_w_value = left_product(inputs, grad_values)
    grad_b_value = jnp.sum(grad_values.astype(jnp.float32), axis=0)
    input_terms = (
        right_product(grad_queries, w_query)
        + right_product(grad_keys, w_key)
        + right_product(grad_values, w_value)
    )
    grad_inputs = grad_resid + lax.psum(input_terms, "tensor")
    grad_grid = grad_inputs.reshape(page_count, page_rows, model_width)
    grad_tokens = jnp.where(replaced, 0.0, grad_grid).reshape(row_count, model_width)
    at_slots = jnp.einsum(
        "pts,ptd->psd", hit_table.astype(jnp.float32), grad_grid, precision=lax.Precision.HIGHEST
    )
    grad_swap_rows = jnp.einsum(
        "psr,psd->rd", pick_table.astype(jnp.float32), at_slots, precision=lax.Precision.HIGHEST
    )
    summed = lax.psum(
        (
            grad_swap_rows,
            grad_w_query,
            grad_b_query,
            grad_w_key,
            grad_w_value,
            grad_b_value,
            grad_w_out,
            grad_b_out,
            grad_first_gain,
            grad_first_shift,
            grad_w_up,
            grad_b_up,
            grad_w_down,
            grad_b_down,
            grad_second_gain,
            grad_second_shift,
        ),
        "dp",
    )
    return (
        to_bf(result),
        grad_tokens,
        summed[0],
        summed[1],
        summed[2],
        summed[3],
        summed[4],
        summed[5],
        summed[6],
        summed[7],
        summed[8],
        summed[9],
        summed[10],
        summed[11],
        summed[12],
        summed[13],
        summed[14],
        summed[15],
    )


def solution(mesh):
    in_specs = (
        P("dp", None),
        P("dp"),
        P("dp", None),
        P("dp", None),
        P(),
        P(None, "tensor"),
        P("tensor"),
        P(None, "tensor"),
        P(None, "tensor"),
        P("tensor"),
        P("tensor", None),
        P(),
        P(),
        P(),
        P(None, "tensor"),
        P("tensor"),
        P("tensor", None),
        P(),
        P(),
        P(),
        P("dp", None),
    )
    out_specs = (
        P("dp", None),
        P("dp", None),
        P(),
        P(None, "tensor"),
        P("tensor"),
        P(None, "tensor"),
        P(None, "tensor"),
        P("tensor"),
        P("tensor", None),
        P(),
        P(),
        P(),
        P(None, "tensor"),
        P("tensor"),
        P("tensor", None),
        P(),
        P(),
        P(),
    )
    return jax.shard_map(local, mesh=mesh, in_specs=in_specs, out_specs=out_specs, check_vma=False)
```

profile of v0, /device:TPU:0, one launch (start us, length us, event | category | flops | bytes accessed | tf_op | source)
XLA Modules:
  0.0 723.7 jit_solution(14196353408719485666)
XLA Ops:
  10.2 1.9 fusion.47
  12.1 2.4 convolution_convert_fusion.5
  14.5 2.3 fusion.52
  18.1 5.9 fusion.127
  24.0 3.6 fusion.58
  29.7 54.0 %all-reduce.10.cloned.1.call-done = f32[512,768]{1,0:T(8,128)} async-done(((f32[512,768]{1,0:T(8,128)}), f32[512,768]{1,0:T(8,128)}) %all-reduce.10.cloned.1.call-update) | async-done | bytes 1572880 | tf_op jit(solution)/shard_map/psum | solution.py:138
  86.1 12.1 %fusion.46 = f32[512,768]{1,0:T(8,128)} fusion(bf16[1536,768]{1,0:T(8,128)(2,1)} %param.37, bf16[768,1536]{1,0:T(8,128)(2,1)S(1)} %copy-done, f32[1536]{0:T(1024)S(1)} %convert_element_type.188, f32[768]{0:T(1024)S(1)} %convert_element_type.186, f32[768]{0:T(1024)S(1)} %convert_element_type.185, f32[512]{0:T(512)S(1)} %add_rsqrt_fusion.3, ...), kind=kOutput, calls=%fused_computation.99 | convolution fusion | flops 2470969344 | bytes 8670208 | tf_op jit(solution)/shard_map/dot_general | solution.py:20
  98.6 51.3 %all-reduce.12.cloned.1.call-done = f32[512,768]{1,0:T(8,128)} async-done(((f32[512,768]{1,0:T(8,128)}), f32[512,768]{1,0:T(8,128)}) %all-reduce.12.cloned.1.call-update) | async-done | bytes 1572880 | tf_op jit(solution)/shard_map/psum | solution.py:145
  149.9 2.5 fusion.126
  163.7 51.6 %all-reduce.14.cloned.1.call-done = f32[512,768]{1,0:T(8,128)} async-done(((f32[512,768]{1,0:T(8,128)}), f32[512,768]{1,0:T(8,128)}) %all-reduce.14.cloned.1.call-update) | async-done | bytes 1572880 | tf_op jit(solution)/shard_map/psum | solution.py:138
  217.3 9.1 %fusion.13 = (bf16[512,1536]{1,0:T(8,128)(2,1)S(1)}, f32[512,1536]{1,0:T(8,128)}) fusion(f32[1536]{0:T(1024)S(1)} %convert_element_type.188, bf16[768,1536]{1,0:T(8,128)(2,1)S(1)} %copy-done, f32[512,768]{1,0:T(8,128)S(1)} %get-tuple-element.121, f32[512]{0:T(512)S(1)} %add_rsqrt_fusion.1, f32[512]{0:T(512)S(1)} %broadcast_multiply_fusion.5, ...), kind=kOutput, calls=%fused_computation.25 | convolution fusion | flops 1261830144 | bytes 8667136 | tf_op jit(solution)/shard_map/dot_general | solution.py:20
  227.6 2.5 fusion.130
  230.2 51.6 %all-reduce.16.cloned.1.call-done = f32[512,768]{1,0:T(8,128)} async-done(((f32[512,768]{1,0:T(8,128)}), f32[512,768]{1,0:T(8,128)}) %all-reduce.16.cloned.1.call-update) | async-done | bytes 1572880 | tf_op jit(solution)/shard_map/psum | solution.py:145
  281.8 2.5 fusion.124
  287.2 3.2 convert_reduce_fusion
  291.6 2.5 fusion.131
  294.6 5.7 fusion.120
  300.3 45.5 %all-reduce.18.cloned.1.call-done = f32[512,768]{1,0:T(8,128)} async-done(((f32[512,768]{1,0:T(8,128)}), f32[512,768]{1,0:T(8,128)}) %all-reduce.18.cloned.1.call-update) | async-done | bytes 1572880 | tf_op jit(solution)/shard_map/psum | solution.py:250
  345.8 3.9 multiply_reduce_fusion.1
  351.4 5.7 convert_reduce_fusion.4
  357.1 4.5 multiply_reduce_fusion
  361.7 4.8 multiply_convert_fusion
  371.7 5.5 fusion.86
  383.7 39.5 %all-reduce.20.cloned.1.call-done = f32[512,768]{1,0:T(8,128)} async-done(((f32[512,768]{1,0:T(8,128)}), f32[512,768]{1,0:T(8,128)}) %all-reduce.20.cloned.1.call-update) | async-done | bytes 1572880 | tf_op jit(solution)/shard_map/psum | solution.py:282
  423.1 2.7 fusion.71
  428.2 64.8 %all-reduce = (f32[384]{0:T(512)}, f32[384]{0:T(512)}, f32[768]{0:T(1024)}, f32[768]{0:T(1024)}, f32[768]{0:T(1024)}, /*index=5*/f32[1536]{0:T(1024)}, f32[768]{0:T(1024)}, f32[768]{0:T(1024)}, f32[768]{0:T(1024)}) all-reduce(f32[384]{0:T(512)S(1)} %reduce_sum.239, ...), channel_id=1, replica_groups=mesh['dp'=16,'tensor'=2] {'dp'}, use_global_device_ids=true, to_apply=%region_27.28 | all-reduce | flops 6912 | bytes 55296 | tf_op jit(solution)/shard_map/psum | solution.py:291
  493.0 3.3 broadcast_select_fusion
  496.3 207.4 %all-reduce.22.cloned.1.call-done = (f32[256,768]{1,0:T(8,128)}, f32[768,384]{1,0:T(8,128)}, f32[768,384]{1,0:T(8,128)}, f32[768,384]{1,0:T(8,128)}, f32[384,768...) async-done(((f32[256,768]{1,0:T(8,128)}, f32[768,384]{1,0:T(8,128)}, f32[768,384]{1,0:T(8,128)}, f32[768,384]{1,0:T(8,128)}, f32[384,768]{1,0:T(8,128)}, ...) | async-done | bytes 14942224 | tf_op jit(solution)/shard_map/psum | solution.py:291
  703.7 2.2 copy.68
  705.9 2.5 copy.69
  712.0 2.2 copy.73
  714.5 2.2 copy.74
  (204 shorter events, 46.3 us)
Async XLA Ops:
  7.2 78.9 %copy-start = (bf16[768,1536]{1,0:T(8,128)(2,1)S(1)}, bf16[768,1536]{1,0:T(8,128)(2,1)}, u32[]{:S(2)}) copy-start(bf16[768,1536]{1,0:T(8,128)(2,1)} %param.35) | copy-start | bytes 7077892
  7.2 76.6 %all-reduce.10.cloned.1.call-start = ((), (), s32[]{:S(2)}) async-start(), calls=%async_computation | async-start | bytes 3145728 | tf_op jit(solution)/shard_map/psum | solution.py:138
  8.8 9.3 %copy-start.54 = (pred[512]{0:T(512)(128)(4,1)}, pred[512]{0:T(512)(128)(4,1)S(1)}, u32[]{:S(2)}) copy-start(pred[512]{0:T(512)(128)(4,1)S(1)} %fusion.75) | copy-start | bytes 1540
  8.8 149.3 %copy-start.36 = (f32[512]{0:T(512)}, f32[512]{0:T(512)S(1)}, u32[]{:S(2)}) copy-start(f32[512]{0:T(512)S(1)} %fusion.82) | copy-start | bytes 6148
  12.1 4.7 copy-start.31
  29.4 120.5 %all-reduce.12.cloned.1.call-start = ((), (), s32[]{:S(2)}) async-start(), calls=%async_computation.1 | async-start | bytes 3145728 | tf_op jit(solution)/shard_map/psum | solution.py:145
  86.1 12.5 %copy-start.50 = (bf16[768]{0:T(1024)(128)(2,1)S(1)}, bf16[768]{0:T(1024)(128)(2,1)}, u32[]{:S(2)}) copy-start(bf16[768]{0:T(1024)(128)(2,1)} %param.39) | copy-start | bytes 4612
  86.1 12.5 %copy-start.51 = (bf16[768]{0:T(1024)(128)(2,1)S(1)}, bf16[768]{0:T(1024)(128)(2,1)}, u32[]{:S(2)}) copy-start(bf16[768]{0:T(1024)(128)(2,1)} %param.38) | copy-start | bytes 4612
  86.1 12.5 %copy-start.52 = (bf16[768]{0:T(1024)(128)(2,1)S(1)}, bf16[768]{0:T(1024)(128)(2,1)}, u32[]{:S(2)}) copy-start(bf16[768]{0:T(1024)(128)(2,1)} %param.40) | copy-start | bytes 4612
  98.3 117.0 %all-reduce.14.cloned.1.call-start = ((), (), s32[]{:S(2)}) async-start(), calls=%async_computation.2 | async-start | bytes 3145728 | tf_op jit(solution)/shard_map/psum | solution.py:138
  163.7 118.1 %all-reduce.16.cloned.1.call-start = ((), (), s32[]{:S(2)}) async-start(), calls=%async_computation.3 | async-start | bytes 3145728 | tf_op jit(solution)/shard_map/psum | solution.py:145
  217.0 9.4 %copy-start.4 = (f32[512,768]{1,0:T(8,128)}, f32[512,768]{1,0:T(8,128)S(1)}, u32[]{:S(2)}) copy-start(f32[512,768]{1,0:T(8,128)S(1)} %get-tuple-element.121) | copy-start | bytes 4718596
  217.3 10.2 %copy-start.57 = (bf16[1536,768]{1,0:T(8,128)(2,1)S(1)}, bf16[1536,768]{1,0:T(8,128)(2,1)}, u32[]{:S(2)}) copy-start(bf16[1536,768]{1,0:T(8,128)(2,1)} %param.37) | copy-start | bytes 7077892
  230.1 115.7 %all-reduce.18.cloned.1.call-start = ((), (), s32[]{:S(2)}) async-start(), calls=%async_computation.4 | async-start | bytes 3145728 | tf_op jit(solution)/shard_map/psum | solution.py:250
  294.2 129.0 %all-reduce.20.cloned.1.call-start = ((), (), s32[]{:S(2)}) async-start(), calls=%async_computation.5 | async-start | bytes 3145728 | tf_op jit(solution)/shard_map/psum | solution.py:282
  345.8 3.9 copy-start.5
  349.7 7.4 %slice-start = ((s8[6291456]{0:T(1024)(128)(4,1)}), s8[4194304]{0:T(1024)(128)(4,1)S(1)}, s32[]{:S(2)}) async-start(s8[6291456]{0:T(1024)(128)(4,1)} %bitcast.85), calls=%async_computation.7 | async-start | bytes 8388608
  350.8 6.3 copy-start.2
  350.8 6.3 slice-start.1
  351.4 5.8 copy-start.35
  361.7 4.8 copy-start.23
  371.5 332.2 %all-reduce.22.cloned.1.call-start = ((), (), s32[]{:S(2)}) async-start(), calls=%async_computation.6 | async-start | bytes 29884416 | tf_op jit(solution)/shard_map/psum | solution.py:291
  371.7 7.2 copy-start.13
  377.3 4.9 copy-start.3
  377.3 4.9 copy-start.19
  380.5 42.6 %copy-start.56 = (s32[1,76]{1,0:T(1,128)S(1)}, s32[1,76]{1,0:T(1,128)}, u32[]{:S(2)}) copy-start(s32[1,76]{1,0:T(1,128)} %param.23) | copy-start | bytes 916
  382.2 43.6 %copy-start.53 = (s32[1,76]{1,0:T(1,128)S(1)}, s32[1,76]{1,0:T(1,128)}, u32[]{:S(2)}) copy-start(s32[1,76]{1,0:T(1,128)} %param.24) | copy-start | bytes 916
  427.4 65.7 %copy-start.55 = (pred[512]{0:T(512)(128)(4,1)S(1)}, pred[512]{0:T(512)(128)(4,1)}, u32[]{:S(2)}) copy-start(pred[512]{0:T(512)(128)(4,1)} %copy-done.54) | copy-start | bytes 1540
  703.7 4.7 copy-start.26
  703.7 5.7 copy-start.25
  705.9 4.5 copy-start.24
  710.4 3.8 slice-start.2
  (40 other events, 72.3 us)
Sparse Core Ops, SparseCore 0:
  29.6 54.1 all-reduce.9
  98.4 51.4 all-reduce.11
  163.8 51.4 all-reduce.13
  230.2 51.4 all-reduce.15
  294.3 51.4 all-reduce.17
  371.6 51.4 all-reduce.19
  429.9 273.7 all-reduce.21
where the time goes:
time: 728 us; the launch traced here: 724 us
  waiting for transfers between devices  501 us (69%)
  matrix products  92 us (13%)
  blocking collectives  64.8 us (9%)
  other arithmetic  30 us (4%)
  local copies, waits for them, and re-layouts  18.8 us (3%)
  between operations  15.9 us (2%)
    psum x1, waiting for transfers between devices, local(): lax.psum((grad_swap_rows, grad_w_query, grad_b_query, grad_w_key, grad_w_...  207 us
    psum x2, waiting for transfers between devices, forward(): branch = lax.psum(product(mixed_heads, w_out), 'tensor') + b_out  106 us
    psum x2, waiting for transfers between devices, forward(): down_out = lax.psum(product(up_act, w_down), 'tensor') + b_down  103 us
    psum x1, blocking collectives, local(): lax.psum((grad_swap_rows, grad_w_query, grad_b_query, grad_w_key, grad_w_...  64.8 us
    psum x1, waiting for transfers between devices, local(): grad_first = grad_second + lax.psum(right_product(grad_pre, w_up), 'tensor')  45.5 us
    psum x1, waiting for transfers between devices, local(): grad_inputs = grad_resid + lax.psum(input_terms, 'tensor')  39.5 us
    dot_general x11, matrix products, product(): return jnp.dot(left, right, preferred_element_type=jnp.float32)  34.8 us
    unnamed x137, local copies, waits for them, and re-layouts  18.6 us
  transfers between devices with their start and end apart: 7, of which 7 were waited for; matrix products, arithmetic and copies ran while one was open for 3% of the time, Pallas kernels for 0%

commit v1 on v0

--- a/solution.py
+++ b/solution.py
@@ -1,7 +1,12 @@
 import jax
 import jax.numpy as jnp
 from jax import lax
+from jax.experimental import pallas as pl
+from jax.experimental.pallas import tpu as pltpu
 from jax.sharding import PartitionSpec as P
+
+F32 = jnp.float32
+MESH = pl.DeviceIdType.MESH
 
 HEAD_DIM = 64
 
@@ -161,6 +166,161 @@
     return (result, kept_values)
 
 
+class Ring:
+    RECV = ("rc", "rya", "rzb", "rza", "rma", "rmb", "ryb", "zoa", "yoa", "mob", "zob", "zoc", "co", "la", "lb")
+    def __init__(self, chunks, eighth, width, offsets=(0,1,2,3,4,5,6,7)):
+        self.offsets=offsets
+        self.n, self.e, self.w = chunks, eighth, width
+    def scratch(self):
+        n,e,w=self.n,self.e,self.w
+        V=lambda *s: pltpu.VMEM(s+(e,w),F32)
+        bufs=[V(n,8), V(n,4), V(n), V(n,2), V(n), V(n), V(n), V(n)]
+        return bufs+[pltpu.SemaphoreType.DMA((len(self.RECV), n)), pltpu.SemaphoreType.DMA((13,))]
+    def bind(self, out, g, rc, rya, rzb, rza, rma, rmb, ryb, recv, sent):
+        self.out,self.g,self.rc,self.rya,self.rzb,self.rza,self.rma,self.rmb,self.ryb=out,g,rc,rya,rzb,rza,rma,rmb,ryb
+        self.recv,self.sent=recv,sent
+        dp=lax.axis_index("dp"); self.dp=dp
+        self.c=dp%2; self.y=(dp//2)%2; self.z=(dp//4)%4
+        self.inner=((self.z+1)//2)==1
+        self.s=self.z//2
+        flip=lambda unit, bit: dp + unit*(1-2*bit)
+        self.to_c=flip(1,self.c); self.to_y=flip(2,self.y); self.to_z=flip(4,self.z%2)
+        self.to_m=dp+4*(3-2*self.z)
+        self.t=lax.axis_index("tensor")
+    def remote(self, name, k, src, dst, to):
+        i=self.RECV.index(name)
+        return pltpu.make_async_remote_copy(src, dst, self.sent.at[i], self.recv.at[i,k], device_id=(to,self.t), device_id_type=MESH)
+    def wait(self, name, k, like):
+        i=self.RECV.index(name)
+        pltpu.make_async_copy(like, like, self.recv.at[i,k]).wait()
+    def local(self, name, k, src, dst):
+        return pltpu.make_async_copy(src, dst, self.recv.at[self.RECV.index(name),k])
+    def barrier(self):
+        bar=pltpu.get_barrier_semaphore()
+        def signal(to): pl.semaphore_signal(bar, inc=1, device_id=(to,self.t), device_id_type=MESH)
+        signal(self.to_c); signal(self.to_y); signal(self.to_z)
+        @pl.when(self.inner)
+        def _():
+            signal(self.to_m)
+            pl.semaphore_wait(bar,4)
+        @pl.when(jnp.logical_not(self.inner))
+        def _():
+            pl.semaphore_wait(bar,3)
+    def half(self,k): return self.out.at[k, pl.ds(self.c*4,4)]
+    def oa(self,k,y): return self.out.at[k, self.c*4+y]
+    def ob(self,k,s): return self.out.at[k, self.c*4+2+s]
+    def stage0(self,k):
+        self.remote("rc",k,self.g.at[k,pl.ds((1-self.c)*4,4)],self.rc.at[k],self.to_c).start()
+    def stage1(self,k):
+        g,c=self.g,self.c
+        self.wait("rc",k,self.rc.at[k])
+        for i in range(4):
+            g[k,c*4+i]=g[k,c*4+i]+self.rc[k,i]
+        self.remote("rya",k,g.at[k,c*4+1-self.y],self.rya.at[k],self.to_y).start()
+        @pl.when(jnp.logical_not(self.inner))
+        def _(): self.remote("rzb",k,g.at[k,pl.ds(c*4+2,2)],self.rzb.at[k],self.to_z).start()
+    def stage2(self,k):
+        g,c,y,s=self.g,self.c,self.y,self.s
+        self.wait("rya",k,self.rya.at[k])
+        g[k,c*4+y]=g[k,c*4+y]+self.rya[k]
+        @pl.when(jnp.logical_not(self.inner))
+        def _(): self.remote("rza",k,g.at[k,c*4+y],self.rza.at[k],self.to_z).start()
+        @pl.when(self.inner)
+        def _():
+            self.wait("rzb",k,self.rzb.at[k])
+            for i in range(2):
+                g[k,c*4+2+i]=g[k,c*4+2+i]+self.rzb[k,i]
+            self.remote("rmb",k,g.at[k,c*4+2+1-s],self.rmb.at[k],self.to_m).start()
+    def stage3(self,k):
+        g,c,y,s=self.g,self.c,self.y,self.s
+        @pl.when(self.inner)
+        def _():
+            self.wait("rza",k,self.rza.at[k])
+            g[k,c*4+y]=g[k,c*4+y]+self.rza[k]
+            self.remote("rma",k,g.at[k,c*4+y],self.rma.at[k],self.to_m).start()
+            self.wait("rmb",k,self.rmb.at[k])
+            g[k,c*4+2+s]=g[k,c*4+2+s]+self.rmb[k]
+            self.remote("ryb",k,g.at[k,c*4+2+s],self.ryb.at[k],self.to_y).start()
+    def stage4(self,k):
+        g,c,y,s=self.g,self.c,self.y,self.s
+        @pl.when(self.inner)
+        def _():
+            self.wait("rma",k,self.rma.at[k])
+            self.rma[k]=self.rma[k]+g[k,c*4+y]
+            self.remote("zoa",k,self.rma.at[k],self.oa(k,y),self.to_z).start()
+            self.remote("yoa",k,self.rma.at[k],self.oa(k,y),self.to_y).start()
+            self.local("la",k,self.rma.at[k],self.oa(k,y)).start()
+            self.wait("ryb",k,self.ryb.at[k])
+            self.ryb[k]=self.ryb[k]+g[k,c*4+2+s]
+            self.remote("mob",k,self.ryb.at[k],self.ob(k,s),self.to_m).start()
+            self.remote("zob",k,self.ryb.at[k],self.ob(k,s),self.to_z).start()
+            self.local("lb",k,self.ryb.at[k],self.ob(k,s)).start()
+    def stage5(self,k):
+        y,s=self.y,self.s
+        @pl.when(jnp.logical_not(self.inner))
+        def _():
+            self.wait("zoa",k,self.oa(k,y))
+            self.remote("yoa",k,self.oa(k,y),self.oa(k,y),self.to_y).start()
+        @pl.when(self.inner)
+        def _():
+            self.wait("mob",k,self.ob(k,1-s))
+            self.remote("zoc",k,self.ob(k,1-s),self.ob(k,1-s),self.to_z).start()
+    def stage6(self,k):
+        y,s=self.y,self.s
+        self.wait("yoa",k,self.oa(k,1-y))
+        @pl.when(self.inner)
+        def _():
+            self.wait("la",k,self.oa(k,y))
+            self.wait("lb",k,self.ob(k,s))
+        @pl.when(jnp.logical_not(self.inner))
+        def _():
+            self.wait("zob",k,self.ob(k,s))
+            self.wait("zoc",k,self.ob(k,1-s))
+        self.remote("co",k,self.half(k),self.half(k),self.to_c).start()
+    def stage7(self,k):
+        self.wait("co",k,self.half(k))
+    def stages(self):
+        return (self.stage7,self.stage6,self.stage5,self.stage4,self.stage3,self.stage2,self.stage1,self.stage0)
+    def tick(self,t):
+        for j,stage in zip(self.offsets[::-1],self.stages()):
+            k=t-j
+            if isinstance(k,int):
+                if 0<=k<self.n: stage(k)
+            else:
+                @pl.when(jnp.logical_and(k>=0,k<self.n))
+                def _(): stage(k)
+    def finish(self):
+        def drain(name, like):
+            i=self.RECV.index(name)
+            pltpu.make_async_copy(like,like,self.sent.at[i]).wait()
+        drain("rc",self.rc); drain("rya",self.rya); drain("yoa",self.rya); drain("co",self.rc)
+        @pl.when(self.inner)
+        def _():
+            for name in ("rmb","rma","ryb","zoa","mob","zob","zoc"): drain(name,self.rya)
+        @pl.when(jnp.logical_not(self.inner))
+        def _():
+            drain("rzb",self.rzb); drain("rza",self.rza)
+
+def comm_only(ring, grads, cid=3):
+    n,e,w=ring.n,ring.e,ring.w
+    def kern(in_ref, out_ref, *scr):
+        *rs, insem = scr
+        ring.bind(out_ref,*rs)
+        for k in range(n): pltpu.make_async_copy(in_ref.at[k], ring.g.at[k], insem.at[k]).start()
+        ring.barrier()
+        def body(t,c):
+            @pl.when(t<n)
+            def _(): pltpu.make_async_copy(in_ref.at[t], ring.g.at[t], insem.at[t]).wait()
+            ring.tick(t)
+            return c
+        lax.fori_loop(0,n+ring.offsets[-1],body,0)
+        ring.finish()
+    return pl.pallas_call(kern, out_shape=jax.ShapeDtypeStruct((n,8,e,w),F32),
+        in_specs=[pl.BlockSpec(memory_space=pl.ANY)], out_specs=pl.BlockSpec(memory_space=pl.ANY),
+        scratch_shapes=ring.scratch()+[pltpu.SemaphoreType.DMA((n,))], name="sum_dp",
+        compiler_params=pltpu.CompilerParams(collective_id=cid, has_side_effects=True, vmem_limit_bytes=60*2**20))(grads)
+
+
 def local(
     tokens,
     lengths,
@@ -183,6 +343,7 @@
     second_gain,
     second_shift,
     cotangent,
+    dp_count,
 ):
     page_count = lengths.shape[0]
     row_count, model_width = tokens.shape
@@ -221,8 +382,6 @@
         second_shift,
     )
     result, kept_values = forward(inputs, lengths, weights_all)
-    inputs_again, unused = lax.optimization_barrier((inputs, result))
-    unused, kept_values = forward(inputs_again, lengths, weights_all)
     (
         queries,
         keys_all,
@@ -282,52 +441,99 @@
     grad_inputs = grad_resid + lax.psum(input_terms, "tensor")
     grad_grid = grad_inputs.reshape(page_count, page_rows, model_width)
     grad_tokens = jnp.where(replaced, 0.0, grad_grid).reshape(row_count, model_width)
-    at_slots = jnp.einsum(
-        "pts,ptd->psd", hit_table.astype(jnp.float32), grad_grid, precision=lax.Precision.HIGHEST
-    )
-    grad_swap_rows = jnp.einsum(
-        "psr,psd->rd", pick_table.astype(jnp.float32), at_slots, precision=lax.Precision.HIGHEST
-    )
-    summed = lax.psum(
-        (
-            grad_swap_rows,
-            grad_w_query,
-            grad_b_query,
-            grad_w_key,
-            grad_w_value,
-            grad_b_value,
+    place_table = product(
+        hit_table[0].astype(jnp.bfloat16), pick_table[0].astype(jnp.bfloat16)
+    )
+    place_table = to_bf(place_table)
+    tensor = lax.axis_index("tensor")
+    half = model_width // 2
+
+    def our_half(value):
+        return lax.dynamic_slice(value, (0, tensor * half), (value.shape[0], half))
+
+    at_half = our_half(grad_inputs)
+    high = to_bf(at_half)
+    low = to_bf(at_half - high.astype(F32))
+    grad_swap = left_product(place_table, high) + left_product(place_table, low)
+    shared = our_half(
+        jnp.stack(
+            [
+                grad_b_out,
+                grad_first_gain,
+                grad_first_shift,
+                grad_b_down,
+                grad_second_gain,
+                grad_second_shift,
+            ]
+        )
+    )
+    private = jnp.concatenate([grad_b_query, grad_b_value, grad_b_up]).reshape(-1, half)
+    heads_width = w_query.shape[1]
+    packed = jnp.concatenate([grad_swap, shared, private], axis=0)
+    packed = packed.reshape(-1, model_width)
+    stack = jnp.concatenate(
+        [
+            grad_w_down,
+            grad_w_up[:, :model_width],
+            grad_w_up[:, model_width:],
             grad_w_out,
-            grad_b_out,
-            grad_first_gain,
-            grad_first_shift,
-            grad_w_up,
-            grad_b_up,
-            grad_w_down,
-            grad_b_down,
-            grad_second_gain,
-            grad_second_shift,
-        ),
-        "dp",
-    )
+            jnp.concatenate([grad_w_query, grad_w_key], axis=1),
+            jnp.concatenate([grad_w_value[:half], grad_w_value[half:]], axis=1),
+            packed,
+        ],
+        axis=0,
+    )
+    eighth = 24
+    rows = stack.shape[0]
+    chunks = -(-rows // (8 * eighth))
+    stack = jnp.pad(stack, ((0, chunks * 8 * eighth - rows), (0, 0)))
+    ring = Ring(chunks, eighth, model_width)
+    summed = comm_only(ring, stack.reshape(chunks, 8, eighth, model_width))
+    summed = summed.reshape(-1, model_width)
+    if dp_count > 16:
+        groups = [list(range(i, dp_count, 16)) for i in range(16)]
+        summed = lax.psum(summed, "dp", axis_index_groups=groups)
+    at = 0
+
+    def take(count):
+        nonlocal at
+        at += count
+        return summed[at - count : at]
+
+    sum_down = take(grad_w_down.shape[0])
+    sum_up = jnp.concatenate([take(model_width), take(model_width)], axis=1)
+    sum_out = take(heads_width)
+    sum_qk = take(model_width)
+    value_part = take(half)
+    sum_value = jnp.concatenate([value_part[:, :half], value_part[:, half:]], axis=0)
+    small = take(packed.shape[0]).reshape(-1, half)
+    repl = swap_rows.shape[0]
+    count = repl + shared.shape[0]
+    both = small[: count + (-count % 8)]
+    other_half = lax.ppermute(both, "tensor", [(0, 1), (1, 0)])
+    left = jnp.where(tensor == 0, both, other_half)
+    right = jnp.where(tensor == 0, other_half, both)
+    whole = jnp.concatenate([left, right], axis=1)
+    vectors = small[count : count + private.shape[0]].reshape(-1)
     return (
         to_bf(result),
         grad_tokens,
-        summed[0],
-        summed[1],
-        summed[2],
-        summed[3],
-        summed[4],
-        summed[5],
-        summed[6],
-        summed[7],
-        summed[8],
-        summed[9],
-        summed[10],
-        summed[11],
-        summed[12],
-        summed[13],
-        summed[14],
-        summed[15],
+        whole[:repl],
+        sum_qk[:, :heads_width],
+        vectors[:heads_width],
+        sum_qk[:, heads_width:],
+        sum_value,
+        vectors[heads_width : 2 * heads_width],
+        sum_out,
+        whole[repl],
+        whole[repl + 1],
+        whole[repl + 2],
+        sum_up,
+        vectors[2 * heads_width :],
+        sum_down,
+        whole[repl + 3],
+        whole[repl + 4],
+        whole[repl + 5],
     )
 
 
@@ -375,4 +581,9 @@
         P(),
         P(),
     )
-    return jax.shard_map(local, mesh=mesh, in_specs=in_specs, out_specs=out_specs, check_vma=False)
+    count = mesh.shape["dp"]
+
+    def run(*arrays):
+        return local(*arrays, dp_count=count)
+
+    return jax.shard_map(run, mesh=mesh, in_specs=in_specs, out_specs=out_specs, check_vma=False)

time: 728 us -> 497 us (0.68)
  waiting for transfers between devices: 501 us -> 192 us
  Pallas kernels: 0 us -> 155 us
  blocking collectives: 64.8 us -> 0 us
  matrix products: 92 us -> 55 us
  local copies, waits for them, and re-layouts: 18.8 us -> 45.1 us
    psum x1 -> x0, waiting for transfers between devices: 207 us -> none  [local(): lax.psum((grad_swap_rows, grad_w_query, grad_b_query, grad_w_key, grad_w_...]
    pallas_call x0 -> x1, Pallas kernels: none -> 155 us  [comm_only(): pl.pallas_call(kern, out_shape=jax.ShapeDtypeStruct((n, 8, e, w), F32), i...]
    psum x1 -> x0, blocking collectives: 64.8 us -> none  [local(): lax.psum((grad_swap_rows, grad_w_query, grad_b_query, grad_w_key, grad_w_...]
    psum x2 -> x1, waiting for transfers between devices: 103 us -> 51 us  [forward(): down_out = lax.psum(product(up_act, w_down), 'tensor') + b_down]
    psum x2 -> x1, waiting for transfers between devices: 106 us -> 54.2 us  [forward(): branch = lax.psum(product(mixed_heads, w_out), 'tensor') + b_out]
    slice x0 -> x12, local copies, waits for them, and re-layouts: none -> 22.5 us  [the longest x3 13.5 us: take(): return summed[at - count:at]]
    dot_general x11 -> x7, matrix products: 34.8 us -> 17.5 us  [product(): return jnp.dot(left, right, preferred_element_type=jnp.float32)]
    pad x0 -> x1, local copies, waits for them, and re-layouts: none -> 11.3 us  [local(): stack = jnp.pad(stack, ((0, chunks * 8 * eighth - rows), (0, 0)))]
  transfers between devices with their start and end apart: 7 -> 5, of which waited for: 7 -> 4; matrix products, arithmetic and copies ran while one was open for 3% -> 6% of each run, Pallas kernels for 0% -> 0%
where the time goes in v1:
time: 497 us; the launch traced here: 496 us
  waiting for transfers between devices  192 us (39%)
  Pallas kernels  155 us (31%)
  matrix products  55 us (11%)
  local copies, waits for them, and re-layouts  45.1 us (9%)
  other arithmetic  33.3 us (7%)
  between operations  15.2 us (3%)
    pallas_call x1, Pallas kernels, comm_only(): pl.pallas_call(kern, out_shape=jax.ShapeDtypeStruct((n, 8, e, w), F32), i...  155 us
    psum x1, waiting for transfers between devices, forward(): branch = lax.psum(product(mixed_heads, w_out), 'tensor') + b_out  54.2 us
    psum x1, waiting for transfers between devices, forward(): down_out = lax.psum(product(up_act, w_down), 'tensor') + b_down  51 us
    psum x1, waiting for transfers between devices, local(): grad_inputs = grad_resid + lax.psum(input_terms, 'tensor')  45.3 us
    psum x1, waiting for transfers between devices, local(): grad_first = grad_second + lax.psum(right_product(grad_pre, w_up), 'tensor')  41 us
    dot_general x7, matrix products, product(): return jnp.dot(left, right, preferred_element_type=jnp.float32)  17.5 us
    slice x3, local copies, waits for them, and re-layouts, take(): return summed[at - count:at]  13.5 us
    dot_general x8, matrix products, left_product(): lax.dot_general(left, right, (((0,), (0,)), ((), ())), preferred_element_...  12.2 us
  transfers between devices with their start and end apart: 5, of which 4 were waited for; matrix products, arithmetic and copies ran while one was open for 6% of the time, Pallas kernels for 0%

profile of v1, /device:TPU:0, one launch (start us, length us, event | category | flops | bytes accessed | tf_op | source)
XLA Modules:
  0.0 496.4 jit_solution(9410449087007632241)
XLA Ops:
  10.2 1.9 fusion.30
  13.7 1.7 fusion.34
  21.6 1.7 fusion.77
  23.4 54.2 %all-reduce.6.cloned.1.call-done = f32[512,768]{1,0:T(8,128)} async-done(((f32[512,768]{1,0:T(8,128)}), f32[512,768]{1,0:T(8,128)}) %all-reduce.6.cloned.1.call-update) | async-done | bytes 1572880 | tf_op jit(solution)/shard_map/psum | solution.py:143
  77.7 1.7 fusion.70
  79.7 9.1 %fusion.6 = (bf16[512,1536]{1,0:T(8,128)(2,1)S(1)}, f32[512,1536]{1,0:T(8,128)}) fusion(f32[1536]{0:T(1024)S(1)} %convert_element_type.164, bf16[768,1536]{1,0:T(8,128)(2,1)S(1)} %copy-done, f32[512,768]{1,0:T(8,128)S(1)} %get-tuple-element.93, f32[768]{0:T(1024)S(1)} %convert_element_type.162, f32[768]{0:T(1024)S(1)} %convert_element_type.161, ...), kind=kOutput, calls=%fused_computation.17 | convolution fusion | flops 1261830144 | bytes 8667136 | tf_op jit(solution)/shard_map/dot_general | solution.py:25
  90.0 2.5 fusion.78
  93.1 51.0 %all-reduce.8.cloned.1.call-done = f32[512,768]{1,0:T(8,128)} async-done(((f32[512,768]{1,0:T(8,128)}), f32[512,768]{1,0:T(8,128)}) %all-reduce.8.cloned.1.call-update) | async-done | bytes 1572880 | tf_op jit(solution)/shard_map/psum | solution.py:150
  144.2 2.5 fusion.69
  150.2 2.7 convert_reduce_fusion
  154.1 2.5 fusion.79
  156.8 5.6 %convolution_dynamic-update-slice_fusion = f32[4742,768]{1,0:T(8,128)} fusion(bf16[512,1536]{1,0:T(8,128)(2,1)} %copy-done.10, f32[512,768]{1,0:T(8,128)} %copy-done.7), kind=kOutput, calls=%fused_computation.10 | convolution fusion | flops 1208352768 | bytes 7864320 | tf_op jit(solution)/shard_map/dot_general | solution.py:29
  162.4 1.6 fusion.65
  165.6 1.6 slice_dynamic-update-slice_fusion
  167.2 41.0 %all-reduce.10.cloned.1.call-done = f32[512,768]{1,0:T(8,128)} async-done(((f32[512,768]{1,0:T(8,128)}), f32[512,768]{1,0:T(8,128)}) %all-reduce.10.cloned.1.call-update) | async-done | bytes 1572880 | tf_op jit(solution)/shard_map/psum | solution.py:409
  208.3 2.8 multiply_reduce_fusion.1
  213.3 4.4 convert_reduce_fusion.4
  217.7 4.5 multiply_reduce_fusion
  222.2 4.8 multiply_convert_fusion
  229.7 1.6 fusion.83
  231.5 2.0 fusion.80
  233.4 1.8 add_add_fusion
  241.6 45.3 %all-reduce.12.cloned.1.call-done = f32[512,768]{1,0:T(8,128)} async-done(((f32[512,768]{1,0:T(8,128)}), f32[512,768]{1,0:T(8,128)}) %all-reduce.12.cloned.1.call-update) | async-done | bytes 1572880 | tf_op jit(solution)/shard_map/psum | solution.py:441
  286.9 2.8 broadcast_select_fusion
  291.3 11.3 %pad.4 = f32[4800,768]{1,0:T(8,128)} pad(f32[4742,768]{1,0:T(8,128)} %constant_dynamic-update-slice_fusion, f32[]{:T(128)} %constant.45.clone.1), padding=0_58x0_0 | pad | bytes 29313028 | tf_op jit(solution)/shard_map/jit(_pad)/pad | solution.py:489
  302.6 155.3 %sum_dp.1 = f32[25,8,24,768]{3,2,1,0:T(8,128)} custom-call(f32[25,8,24,768]{3,2,1,0:T(8,128)} %bitcast.75), custom_call_target="tpu_custom_call" | custom-call | tf_op jit(solution)/shard_map/sum_dp/pallas_call | solution.py:318
  457.9 5.8 %fusion.71 = (f32[4,8,24,768]{3,2,1,0:T(8,128)}, f32[4,8,24,768]{3,2,1,0:T(8,128)}, f32[4,8,24,768]{3,2,1,0:T(8,128)S(1)}) fusion(f32[25,8,24,768]{3,2,1,0:T(8,128)} %sum_dp.1), kind=kLoop, calls=%fused_computation.156 | loop fusion | bytes 14155776 | tf_op jit(solution)/shard_map/slice | solution.py:501
  463.6 2.9 fusion.72
  466.5 1.8 slice.145
  469.0 1.8 slice.112
  475.8 4.9 slice.136
  482.0 5.2 %pad_maximum_fusion = f32[768,1536]{1,0:T(8,128)} fusion(f32[768,768]{1,0:T(8,128)} %bitcast.81, f32[768,768]{1,0:T(8,128)} %bitcast.80), kind=kLoop, calls=%fused_computation.9 | loop fusion | flops 1179648 | bytes 9437184 | tf_op jit(solution)/shard_map/concatenate | solution.py:504
  (166 shorter events, 40.9 us)
Async XLA Ops:
  7.2 72.5 %copy-start = (bf16[768,1536]{1,0:T(8,128)(2,1)S(1)}, bf16[768,1536]{1,0:T(8,128)(2,1)}, u32[]{:S(2)}) copy-start(bf16[768,1536]{1,0:T(8,128)(2,1)} %param.35) | copy-start | bytes 7077892
  7.2 70.4 %all-reduce.6.cloned.1.call-start = ((), (), s32[]{:S(2)}) async-start(), calls=%async_computation | async-start | bytes 3145728 | tf_op jit(solution)/shard_map/psum | solution.py:143
  13.7 3.0 copy-start.18
  16.7 2.6 copy-start.2
  20.8 2.6 copy-start.28
  20.8 2.6 copy-start.29
  20.8 2.6 copy-start.30
  20.8 2.6 copy-start.27
  23.3 120.9 %all-reduce.8.cloned.1.call-start = ((), (), s32[]{:S(2)}) async-start(), calls=%async_computation.1 | async-start | bytes 3145728 | tf_op jit(solution)/shard_map/psum | solution.py:150
  79.3 9.4 %copy-start.3 = (f32[512,768]{1,0:T(8,128)}, f32[512,768]{1,0:T(8,128)S(1)}, u32[]{:S(2)}) copy-start(f32[512,768]{1,0:T(8,128)S(1)} %get-tuple-element.93) | copy-start | bytes 4718596
  79.7 10.3 %copy-start.36 = (bf16[1536,768]{1,0:T(8,128)(2,1)S(1)}, bf16[1536,768]{1,0:T(8,128)(2,1)}, u32[]{:S(2)}) copy-start(bf16[1536,768]{1,0:T(8,128)(2,1)} %param.37) | copy-start | bytes 7077892
  90.0 2.8 copy-start.31
  90.0 2.8 copy-start.32
  90.0 2.9 copy-start.33
  90.0 2.9 copy-start.34
  90.0 2.9 copy-start.35
  92.5 115.7 %all-reduce.10.cloned.1.call-start = ((), (), s32[]{:S(2)}) async-start(), calls=%async_computation.2 | async-start | bytes 3145728 | tf_op jit(solution)/shard_map/psum | solution.py:409
  144.2 2.8 copy-start.9
  147.0 2.4 copy-start.40
  149.4 3.4 copy-start.7
  156.6 130.3 %all-reduce.12.cloned.1.call-start = ((), (), s32[]{:S(2)}) async-start(), calls=%async_computation.3 | async-start | bytes 3145728 | tf_op jit(solution)/shard_map/psum | solution.py:441
  156.7 5.6 %copy-start.4 = (f32[512,768]{1,0:T(8,128)S(1)}, f32[512,768]{1,0:T(8,128)}, u32[]{:S(2)}) copy-start(f32[512,768]{1,0:T(8,128)} %copy-done.3) | copy-start | bytes 4718596
  156.8 5.6 %copy-start.39 = (bf16[512,1536]{1,0:T(8,128)(2,1)S(1)}, bf16[512,1536]{1,0:T(8,128)(2,1)}, u32[]{:S(2)}) copy-start(bf16[512,1536]{1,0:T(8,128)(2,1)} %copy-done.38) | copy-start | bytes 4718596
  208.3 4.5 copy-start.12
  211.1 6.6 %slice-start = ((s8[6291456]{0:T(1024)(128)(4,1)}), s8[4194304]{0:T(1024)(128)(4,1)S(1)}, s32[]{:S(2)}) async-start(s8[6291456]{0:T(1024)(128)(4,1)} %bitcast.73), calls=%async_computation.4 | async-start | bytes 8388608
  212.8 4.9 slice-start.1
  213.3 4.4 copy-start.26
  222.2 4.8 copy-start.19
  235.4 2.8 copy-start.8
  470.9 16.4 %collective-permute-start = (f32[264,384]{1,0:T(8,128)}, f32[264,384]{1,0:T(8,128)}, u32[]{:S(2)}, u32[]{:S(2)}) collective-permute-start(f32[264,384]{1,0:T(8,128)} %slice.112), channel_id=1, source_target_pairs={{0,1},{1,0},{2,3},{3,2},{4,5},{5,4},{6,7},{7,6},{8,9},{9,8},{10,11... | collective-permute-start | bytes 1216520 | tf_op jit(solution)/shard_map/ppermute | solution.py:513
  482.0 5.2 %copy-start.15 = (f32[264,384]{1,0:T(8,128)S(1)}, f32[264,384]{1,0:T(8,128)}, u32[]{:S(2)}) copy-start(f32[264,384]{1,0:T(8,128)} %slice.112) | copy-start | bytes 1216516
  482.0 7.9 %copy-start.1 = (bf16[768,1536]{1,0:T(8,128)(2,1)S(1)}, bf16[768,1536]{1,0:T(8,128)(2,1)}, u32[]{:S(2)}) copy-start(bf16[768,1536]{1,0:T(8,128)(2,1)} %param.35) | copy-start | bytes 7077892
  (16 other events, 24.8 us)
Sparse Core Ops, SparseCore 0:
  23.4 54.1 all-reduce.5
  92.7 51.4 all-reduce.7
  156.8 51.4 all-reduce.9
  235.4 51.4 all-reduce.11

commit v2 on v1

--- a/solution.py
+++ b/solution.py
@@ -52,118 +52,6 @@
         - jnp.mean(scaled, axis=-1, keepdims=True)
         - normed * jnp.mean(scaled * normed, axis=-1, keepdims=True)
     )
-
-
-def gelu_slope(pre_act):
-    return (
-        0.5 * (1.0 + lax.erf(pre_act * half_root))
-        + pre_act * jnp.exp(-0.5 * pre_act * pre_act) * gauss_norm
-    )
-
-
-def page_scores(queries, keys_page, length):
-    key_bias = jnp.where(jnp.arange(keys_page.shape[0]) < length, 0.0, mask_fill).astype(
-        jnp.float32
-    )
-    scores = jnp.einsum("qhe,khe->hqk", queries, keys_page, preferred_element_type=jnp.float32)
-    return scores + key_bias[None, None, :]
-
-
-def page_forward(page_block):
-    queries, keys_page, values_page, length = page_block
-    scores = page_scores(queries, keys_page, length)
-    row_max = jnp.max(scores, axis=-1, keepdims=True)
-    exponent = jnp.exp(scores - row_max)
-    row_total = jnp.sum(exponent, axis=-1, keepdims=True)
-    probs_low = to_bf(exponent / row_total)
-    mixed_page = jnp.einsum(
-        "hqk,khe->qhe", probs_low, values_page, preferred_element_type=jnp.float32
-    )
-    return (mixed_page, (row_max + jnp.log(row_total))[:, :, 0])
-
-
-def page_backward(page_block):
-    queries, keys_page, values_page, length, log_total, grad_mixed = page_block
-    scores = page_scores(queries, keys_page, length)
-    probs = jnp.exp(scores - log_total[:, :, None])
-    grad_probs = jnp.einsum(
-        "qhe,khe->hqk", grad_mixed, values_page, preferred_element_type=jnp.float32
-    )
-    grad_scores = to_bf(probs * (grad_probs - jnp.sum(probs * grad_probs, axis=-1, keepdims=True)))
-    grad_queries = to_bf(
-        jnp.einsum("hqk,khe->qhe", grad_scores, keys_page, preferred_element_type=jnp.float32)
-    )
-    grad_keys = to_bf(
-        jnp.einsum("hqk,qhe->khe", grad_scores, queries, preferred_element_type=jnp.float32)
-    )
-    grad_values = to_bf(
-        jnp.einsum("hqk,qhe->khe", to_bf(probs), grad_mixed, preferred_element_type=jnp.float32)
-    )
-    return (grad_queries, grad_keys, grad_values)
-
-
-def split_pages(flat_part, page_count):
-    return flat_part.reshape(page_count, -1, flat_part.shape[1] // HEAD_DIM, HEAD_DIM)
-
-
-def forward(inputs, lengths, weights_all):
-    (
-        w_query,
-        b_query,
-        w_key,
-        w_value,
-        b_value,
-        w_out,
-        b_out,
-        first_gain,
-        first_shift,
-        w_up,
-        b_up,
-        w_down,
-        b_down,
-        second_gain,
-        second_shift,
-    ) = weights_all
-    page_count = lengths.shape[0]
-    row_count = inputs.shape[0]
-    query_scale = HEAD_DIM ** (-0.5)
-    queries = to_bf((product(inputs, w_query) + b_query) * query_scale)
-    keys_all = to_bf(product(inputs, w_key))
-    values_all = to_bf(product(inputs, w_value) + b_value)
-    mixed_heads, log_total = lax.map(
-        page_forward,
-        (
-            split_pages(queries, page_count),
-            split_pages(keys_all, page_count),
-            split_pages(values_all, page_count),
-            lengths,
-        ),
-    )
-    mixed_heads = to_bf(mixed_heads.reshape(row_count, -1))
-    branch = lax.psum(product(mixed_heads, w_out), "tensor") + b_out
-    first_out, first_normed, first_inv = layer_norm(
-        inputs.astype(jnp.float32) + branch, first_gain, first_shift
-    )
-    first_low = to_bf(first_out)
-    up_pre = product(first_low, w_up) + b_up
-    up_act = to_bf(jax.nn.gelu(up_pre, approximate=False))
-    down_out = lax.psum(product(up_act, w_down), "tensor") + b_down
-    result, second_normed, second_inv = layer_norm(first_out + down_out, second_gain, second_shift)
-    kept_values = (
-        queries,
-        keys_all,
-        values_all,
-        mixed_heads,
-        log_total,
-        first_normed,
-        first_inv,
-        first_low,
-        up_pre,
-        up_act,
-        second_normed,
-        second_inv,
-    )
-    return (result, kept_values)
 
 
 class Ring:
@@ -321,6 +209,380 @@
         compiler_params=pltpu.CompilerParams(collective_id=cid, has_side_effects=True, vmem_limit_bytes=60*2**20))(grads)
 
 
+class Forward:
+    PARTS = 4
+    SENDS = ("x", "z", "y", "cx", "cz", "cy")
+
+    def __init__(self, rows, width, heads_width, hidden):
+        self.rows, self.width, self.heads_width, self.hidden = rows, width, heads_width, hidden
+        self.heads = heads_width // HEAD_DIM
+        self.third_hidden = hidden // 3
+        self.blocks = hidden // 256
+        self.per_core = self.third_hidden // 256
+        self.panels = 2 + 2 * self.per_core
+        self.chunks = self.panels * self.PARTS
+        self.part_rows = width // self.PARTS
+
+    def outs(self):
+        r, w, hw, hid = self.rows, self.width, self.heads_width, self.hidden
+        bf = jnp.bfloat16
+        S = jax.ShapeDtypeStruct
+        return dict(
+            layer=S((r, w), bf),
+            wq=S((w, hw), bf), wk=S((w, hw), bf), wv=S((w, hw), bf), wo=S((hw, w), bf),
+            wu=S((w, hid), bf), wd=S((hid, w), bf),
+            inp=S((r, w), bf), place=S((r, 256), bf),
+            q=S((2 * self.heads, r, HEAD_DIM), bf), k=S((2 * self.heads, r, HEAD_DIM), bf),
+            v=S((2 * self.heads, r, HEAD_DIM), bf), lse=S((2 * self.heads, 1, r), F32),
+            mixed=S((r, hw), bf),
+            first_low=S((r, w), bf), first_normed=S((r, w), F32), first_inv=S((r, 1), F32),
+            act=S((self.blocks, r, 256), bf), slope=S((2 * self.blocks, r, 256), bf),
+            grad_second=S((r, w), F32), grad_down=S((r, w), bf), sums=S((8, w), F32),
+        )
+
+    def call(self, *args):
+        outs = self.outs()
+        names = list(outs)
+        n = self.chunks
+        panel = pltpu.VMEM((n, self.part_rows, 128), F32)
+        scratch = [pltpu.VMEM(o.shape, o.dtype) for o in outs.values()]
+        scratch += [panel] * 7
+        scratch += [
+            pltpu.VMEM((8, 2 * self.heads_width + self.hidden), F32),
+            pltpu.VMEM((self.rows, self.width), F32),
+            pltpu.VMEM((self.rows, self.width), F32),
+            pltpu.VMEM((self.rows, self.width), F32),
+            pltpu.SemaphoreType.DMA((len(self.SENDS), n)),
+            pltpu.SemaphoreType.DMA((len(self.SENDS) + 1,)),
+            pltpu.SemaphoreType.DMA((1,)),
+            pltpu.SemaphoreType.DMA((len(names),)),
+        ]
+        vm = pl.BlockSpec(memory_space=pltpu.VMEM)
+        specs = [pl.BlockSpec(memory_space=pltpu.SMEM)] + [vm] * (len(args) - 1)
+
+        def kern(*refs):
+            ins = refs[: len(args)]
+            out_refs = dict(zip(names, refs[len(args) : len(args) + len(names)]))
+            rest = refs[len(args) + len(names) :]
+            held = dict(zip(names, rest[: len(names)]))
+            self.body(ins, out_refs, held, *rest[len(names) :])
+
+        got = pl.pallas_call(
+            kern,
+            out_shape=tuple(outs.values()),
+            in_specs=specs,
+            out_specs=tuple(pl.BlockSpec(memory_space=pl.ANY) for _ in names),
+            scratch_shapes=scratch,
+            name="forward_gather",
+            compiler_params=pltpu.CompilerParams(
+                collective_id=4, has_side_effects=True, vmem_limit_bytes=62 * 2**20
+            ),
+        )(*args)
+        return dict(zip(names, got))
+
+    def body(self, ins, out_refs, held, xs, lx, lz, ly, sx, sz, sy, bias_o, acc, acc_o, first_out, recv, sent, brecv, saved):
+        (length, tokens, positions, swap_ids, swap_rows, wq, wk, wv, wo, wu, wd, bias, vectors, cot) = ins
+        rows, width, hw, hidden = self.rows, self.width, self.heads_width, self.hidden
+        n, parts, part_rows = self.chunks, self.PARTS, self.part_rows
+        bf = jnp.bfloat16
+        dp = lax.axis_index("dp")
+        tensor = lax.axis_index("tensor")
+        c, y, low = dp % 2, (dp // 2) % 2, (dp // 4) % 2
+
+        def flip(unit, bit):
+            return dp + unit * (1 - 2 * bit)
+
+        to = {"x": (dp, 1 - tensor), "z": (flip(4, low), tensor), "y": (flip(2, y), tensor)}
+        to["cx"] = to["cz"] = to["cy"] = (flip(1, c), tensor)
+        own_third = jnp.where(low == 0, y, 2)
+        z_third = jnp.where(low == 0, 2, y)
+        y_third = 1 - y
+
+        def remote(name, i, src, dst):
+            s = self.SENDS.index(name)
+            return pltpu.make_async_remote_copy(
+                src.at[i], dst.at[i], sent.at[s], recv.at[s, i], device_id=to[name], device_id_type=MESH
+            )
+
+        def wait(name, i, dst):
+            pltpu.make_async_copy(dst.at[i], dst.at[i], recv.at[self.SENDS.index(name), i]).wait()
+
+        def save(name):
+            pltpu.make_async_copy(
+                held[name], out_refs[name], saved.at[list(held).index(name)]
+            ).start()
+
+        bar = pltpu.get_barrier_semaphore()
+        for name in ("x", "z", "y", "cx"):
+            pl.semaphore_signal(bar, inc=1, device_id=to[name], device_id_type=MESH)
+
+        def put(p, value):
+            xs[p * parts : (p + 1) * parts] = value.astype(F32).reshape(parts, part_rows, 128)
+
+        def put_blocks(p, ref, at):
+            for b in range(width // 128):
+                lo = b * 128
+                block = ref[pl.ds(pl.multiple_of(at, 128), 128), lo : lo + 128].astype(F32)
+                done = 0
+                while done < 128:
+                    i, r = divmod(lo + done, part_rows)
+                    take = min(128 - done, part_rows - r)
+                    xs[p * parts + i, r : r + take] = block[done : done + take]
+                    done += take
+
+        def start_x(p):
+            for i in range(p * parts, (p + 1) * parts):
+                remote("x", i, xs, lx).start()
+
+        def col(at):
+            return pl.ds(pl.multiple_of(at, 128), 128)
+
+        at = own_third * 128
+
+        @pl.when(c == 0)
+        def _():
+            put(0, wq[:, col(at)])
+            put(1, wk[:, col(at)])
+
+        @pl.when(c == 1)
+        def _():
+            put(0, wv[:, col(at)])
+            put_blocks(1, wo, at)
+
+        pl.semaphore_wait(bar, 4)
+        pltpu.make_async_remote_copy(
+            bias, bias_o, sent.at[len(self.SENDS)], brecv.at[0], device_id=to["x"], device_id_type=MESH
+        ).start()
+        start_x(0)
+        start_x(1)
+        pc = self.per_core
+        for j in range(pc):
+            put(2 + j, wu[:, col(own_third * self.third_hidden + (pc * c + j) * 128)])
+            start_x(2 + j)
+        for j in range(pc):
+            put_blocks(2 + pc + j, wd, own_third * self.third_hidden + (pc * c + j) * 128)
+            start_x(2 + pc + j)
+
+        def relay_x(i):
+            wait("x", i, lx)
+            remote("z", i, lx, lz).start()
+            remote("cx", i, lx, sx).start()
+
+            @pl.when(low == 0)
+            def _():
+                remote("y", i, lx, ly).start()
+
+        def relay_z(i):
+            wait("z", i, lz)
+            remote("cz", i, lz, sz).start()
+
+            @pl.when(low == 1)
+            def _():
+                remote("y", i, lz, ly).start()
+
+        def relay_y(i):
+            wait("y", i, ly)
+            remote("cy", i, ly, sy).start()
+
+        def tick(t):
+            for relay, k in ((relay_x, t), (relay_z, t - 1), (relay_y, t - 2)):
+                if isinstance(k, int):
+                    if 0 <= k < n:
+                        relay(k)
+                else:
+
+                    @pl.when(jnp.logical_and(k >= 0, k < n))
+                    def _():
+                        relay(k)
+
+        place_rows = lax.broadcasted_iota(jnp.int32, (rows, positions.shape[1]), 0)
+        hit = jnp.where(place_rows == positions[...], 1.0, 0.0).astype(bf)
+        repl_rows = lax.broadcasted_iota(jnp.int32, (swap_rows.shape[0], positions.shape[1]), 0)
+        chosen = jnp.where(repl_rows == swap_ids[...], 1.0, 0.0).astype(bf)
+        place = right_product(hit, chosen)
+        held["place"][...] = to_bf(place)
+        save("place")
+        swapped = product(held["place"][...], swap_rows[...])
+        is_swapped = jnp.sum(place, axis=1, keepdims=True) > 0.5
+        held["inp"][...] = to_bf(jnp.where(is_swapped, swapped, tokens[...].astype(F32)))
+        save("inp")
+        tick(0)
+        inp = held["inp"]
+        scale = HEAD_DIM ** (-0.5)
+        qh, kh, vh, lse = held["q"], held["k"], held["v"], held["lse"]
+        heads = self.heads
+
+        def project(first_head, w_q, w_k, w_v, b_ref):
+            part = to_bf((product(inp[...], w_q[...]) + b_ref[0:1, :hw]) * scale)
+            for h in range(heads):
+                qh[first_head + h] = part[:, h * HEAD_DIM : (h + 1) * HEAD_DIM]
+            part = to_bf(product(inp[...], w_k[...]))
+            for h in range(heads):
+                kh[first_head + h] = part[:, h * HEAD_DIM : (h + 1) * HEAD_DIM]
+            part = to_bf(product(inp[...], w_v[...]) + b_ref[0:1, hw : 2 * hw])
+            for h in range(heads):
+                vh[first_head + h] = part[:, h * HEAD_DIM : (h + 1) * HEAD_DIM]
+
+        key_bias = jnp.where(
+            lax.broadcasted_iota(jnp.int32, (rows, 1), 0) < length[0], 0.0, mask_fill
+        ).astype(F32)
+
+        def attend(h):
+            scores = right_product(kh[h], qh[h]) + key_bias
+            top = jnp.max(scores, axis=0, keepdims=True)
+            exponent = jnp.exp(scores - top)
+            total = jnp.sum(exponent, axis=0, keepdims=True)
+            lse[h] = top + jnp.log(total)
+            probs = to_bf(exponent * (1.0 / total))
+            return to_bf(left_product(probs, vh[h]))
+
+        def attend_pairs(first_head, mixed_ref, t0):
+            for p in range(heads // 2):
+                tick(t0 + 2 * p)
+                one = attend(first_head + 2 * p)
+                tick(t0 + 2 * p + 1)
+                two = attend(first_head + 2 * p + 1)
+                mixed_ref[:, p * 128 : (p + 1) * 128] = jnp.concatenate([one, two], axis=1)
+
+        project(0, wq, wk, wv, bias)
+        tick(1)
+        tick(2)
+        attend_pairs(0, held["mixed"], 3)
+        save("mixed")
+        acc[...] = product(held["mixed"][...], wo[...])
+        attn = 2 * parts
+        t = 3 + heads
+        while t < attn + 2:
+            tick(t)
+            t += 1
+        thirds = ((own_third, lx, sx, "cx"), (z_third, lz, sz, "cz"), (y_third, ly, sy, "cy"))
+
+        def panel_of(ref, p):
+            return to_bf(ref[p * parts : (p + 1) * parts].reshape(width, 128))
+
+        def unblock(ref, value, at):
+            for b in range(width // 128):
+                ref[pl.ds(pl.multiple_of(at, 128), 128), b * 128 : (b + 1) * 128] = value[
+                    b * 128 : (b + 1) * 128
+                ]
+
+        for third, mine, theirs, name in thirds:
+            for i in range(attn):
+                wait(name, i, theirs)
+
+            def assemble(first, second):
+                held["wq"][:, col(third * 128)] = panel_of(first, 0)
+                held["wk"][:, col(third * 128)] = panel_of(first, 1)
+                held["wv"][:, col(third * 128)] = panel_of(second, 0)
+                unblock(held["wo"], panel_of(second, 1), third * 128)
+
+            @pl.when(c == 0)
+            def _():
+                assemble(mine, theirs)
+
+            @pl.when(c == 1)
+            def _():
+                assemble(theirs, mine)
+
+        for name in ("wq", "wk", "wv", "wo"):
+            save(name)
+        pltpu.make_async_copy(bias_o, bias_o, brecv.at[0]).wait()
+        tick(t)
+        t += 1
+        project(heads, held["wq"], held["wk"], held["wv"], bias_o)
+        mixed_o = first_out
+        other_parts = []
+        for p in range(heads // 2):
+            tick(t)
+            one = attend(heads + 2 * p)
+            tick(t + 1)
+            two = attend(heads + 2 * p + 1)
+            t += 2
+            mixed_o[:, p * 128 : (p + 1) * 128] = jnp.concatenate([one, two], axis=1).astype(F32)
+        for name in ("q", "k", "v", "lse"):
+            save(name)
+        acc_o[...] = product(to_bf(mixed_o[:, :hw]), held["wo"][...])
+        branch = (acc[...] + acc_o[...]) + vectors[0:1]
+        first, normed, inv = layer_norm(inp[...].astype(F32) + branch, vectors[1:2], vectors[2:3])
+        first_out[...] = first
+        held["first_low"][...] = to_bf(first)
+        held["first_normed"][...] = normed
+        held["first_inv"][...] = inv
+        for name in ("first_low", "first_normed", "first_inv"):
+            save(name)
+        tick(t)
+        t += 1
+        act, slope = held["act"], held["slope"]
+
+        def feed(b, at, w_ref, b_ref):
+            up = (
+                product(held["first_low"][...], w_ref[:, b * 256 : (b + 1) * 256])
+                + b_ref[0:1, 2 * hw + b * 256 : 2 * hw + (b + 1) * 256]
+            )
+            cdf = 0.5 * (1.0 + lax.erf(up * half_root))
+            slope[at] = to_bf(cdf + up * jnp.exp(-0.5 * up * up) * gauss_norm)
+            return to_bf(up * cdf)
+
+        for b in range(self.blocks):
+            act[b] = feed(b, b, wu, bias)
+            tick(t)
+            t += 1
+        save("act")
+        acc[...] = product(act[0], wd[0:256])
+        for b in range(1, self.blocks):
+            acc[...] += product(act[b], wd[b * 256 : (b + 1) * 256])
+        while t < n + 2:
+            tick(t)
+            t += 1
+        for third, mine, theirs, name in thirds:
+            for i in range(attn, attn + pc * parts):
+                wait(name, i, theirs)
+            for j in range(pc):
+                at = third * self.third_hidden + (pc * c + j) * 128
+                held["wu"][:, col(at)] = panel_of(mine, 2 + j)
+                at = third * self.third_hidden + (pc * (1 - c) + j) * 128
+                held["wu"][:, col(at)] = panel_of(theirs, 2 + j)
+        save("wu")
+        other_act = []
+        for b in range(self.blocks):
+            other_act.append(feed(b, self.blocks + b, held["wu"], bias_o))
+        save("slope")
+        for third, mine, theirs, name in thirds:
+            for i in range(attn + pc * parts, n):
+                wait(name, i, theirs)
+            for j in range(pc):
+                at = third * self.third_hidden + (pc * c + j) * 128
+                unblock(held["wd"], panel_of(mine, 2 + pc + j), at)
+                at = third * self.third_hidden + (pc * (1 - c) + j) * 128
+                unblock(held["wd"], panel_of(theirs, 2 + pc + j), at)
+        save("wd")
+        acc_o[...] = product(other_act[0], held["wd"][0:256])
+        for b in range(1, self.blocks):
+            acc_o[...] += product(other_act[b], held["wd"][b * 256 : (b + 1) * 256])
+        down = (acc[...] + acc_o[...]) + vectors[3:4]
+        result, normed, inv = layer_norm(first_out[...] + down, vectors[4:5], vectors[5:6])
+        held["layer"][...] = to_bf(result)
+        save("layer")
+        grad_out = cot[...].astype(F32)
+        grad = norm_back(grad_out, normed, inv, vectors[4:5])
+        held["grad_second"][...] = grad
+        save("grad_second")
+        low_grad = to_bf(grad)
+        held["grad_down"][...] = low_grad
+        save("grad_down")
+        sums = held["sums"]
+        sums[...] = jnp.zeros_like(sums)
+        sums[0:1] = jnp.sum(grad_out * normed, axis=0, keepdims=True)
+        sums[1:2] = jnp.sum(grad_out, axis=0, keepdims=True)
+        sums[2:3] = jnp.sum(low_grad.astype(F32), axis=0, keepdims=True)
+        save("sums")
+        for name, like in (("x", xs), ("z", lx), ("y", lx), ("cx", lx), ("cz", lx), ("cy", lx)):
+            pltpu.make_async_copy(like, like, sent.at[self.SENDS.index(name)]).wait()
+        pltpu.make_async_copy(bias_o, bias_o, sent.at[len(self.SENDS)]).wait()
+        for i, name in enumerate(held):
+            pltpu.make_async_copy(held[name], out_refs[name], saved.at[i]).wait()
+
+
 def local(
     tokens,
     lengths,
@@ -345,106 +607,80 @@
     cotangent,
     dp_count,
 ):
-    page_count = lengths.shape[0]
     row_count, model_width = tokens.shape
-    page_rows = row_count // page_count
-    hit_table = positions[:, None, :] == jnp.arange(page_rows)[None, :, None]
-    pick_table = swap_ids[:, :, None] == jnp.arange(swap_rows.shape[0])[None, None, :]
-    chosen = to_bf(
-        jnp.einsum(
-            "psr,rd->psd",
-            pick_table.astype(jnp.bfloat16),
-            swap_rows,
-            preferred_element_type=jnp.float32,
-        )
+    heads_width = w_query.shape[1]
+    hidden = w_up.shape[1]
+    bias = jnp.concatenate([b_query, b_value, b_up]).astype(F32)
+    bias = jnp.broadcast_to(bias[None, :], (8, bias.shape[0]))
+    vectors = jnp.stack(
+        [b_out, first_gain, first_shift, b_down, second_gain, second_shift, b_out, b_out]
+    ).astype(F32)
+    fw = Forward(row_count, model_width, heads_width, hidden).call(
+        lengths, tokens, positions, swap_ids, swap_rows, w_query, w_key, w_value, w_out, w_up, w_down,
+        bias, vectors, cotangent,
     )
-    placed = jnp.einsum(
-        "pts,psd->ptd", hit_table.astype(jnp.bfloat16), chosen, preferred_element_type=jnp.float32
-    )
-    replaced = jnp.any(hit_table, axis=-1)[:, :, None]
-    inputs = jnp.where(replaced, to_bf(placed), tokens.reshape(page_count, page_rows, model_width))
-    inputs = inputs.reshape(row_count, model_width)
-    weights_all = (
-        w_query,
-        b_query,
-        w_key,
-        w_value,
-        b_value,
-        w_out,
-        b_out,
-        first_gain,
-        first_shift,
-        w_up,
-        b_up,
-        w_down,
-        b_down,
-        second_gain,
-        second_shift,
-    )
-    result, kept_values = forward(inputs, lengths, weights_all)
-    (
-        queries,
-        keys_all,
-        values_all,
-        mixed_heads,
-        log_total,
-        first_normed,
-        first_inv,
-        first_low,
-        up_pre,
-        up_act,
-        second_normed,
-        second_inv,
-    ) = kept_values
-    grad_out = cotangent.astype(jnp.float32)
-    grad_second_gain = jnp.sum(grad_out * second_normed, axis=0)
-    grad_second_shift = jnp.sum(grad_out, axis=0)
-    grad_second = norm_back(grad_out, second_normed, second_inv, second_gain)
-    grad_down = to_bf(grad_second)
-    grad_b_down = jnp.sum(grad_down.astype(jnp.float32), axis=0)
-    grad_w_down = left_product(up_act, grad_down)
-    grad_pre = to_bf(right_product(grad_down, w_down) * gelu_slope(up_pre))
-    grad_b_up = jnp.sum(grad_pre.astype(jnp.float32), axis=0)
-    grad_w_up = left_product(first_low, grad_pre)
-    grad_first = grad_second + lax.psum(right_product(grad_pre, w_up), "tensor")
+    result = fw["layer"]
+    place_table = fw["place"]
+    inputs = fw["inp"]
+    heads = heads_width // HEAD_DIM
+    grad_second_gain, grad_second_shift, grad_b_down = fw["sums"][0], fw["sums"][1], fw["sums"][2]
+    grad_second, grad_down = fw["grad_second"], fw["grad_down"]
+    blocks = hidden // 256
+    act_own = fw["act"].transpose(1, 0, 2).reshape(row_count, hidden)
+    slope_own = fw["slope"][:blocks].transpose(1, 0, 2).reshape(row_count, hidden)
+    slope_other = fw["slope"][blocks:].transpose(1, 0, 2).reshape(row_count, hidden)
+    first_low, first_normed, first_inv = fw["first_low"], fw["first_normed"], fw["first_inv"]
+    grad_w_down = left_product(act_own, grad_down)
+    pre_own = to_bf(right_product(grad_down, w_down) * slope_own)
+    pre_other = to_bf(right_product(grad_down, fw["wd"]) * slope_other)
+    grad_b_up = jnp.sum(pre_own.astype(F32), axis=0)
+    grad_w_up = left_product(first_low, pre_own)
+    grad_first = grad_second + (right_product(pre_own, w_up) + right_product(pre_other, fw["wu"]))
     grad_first_gain = jnp.sum(grad_first * first_normed, axis=0)
     grad_first_shift = jnp.sum(grad_first, axis=0)
     grad_resid = norm_back(grad_first, first_normed, first_inv, first_gain)
     grad_branch = to_bf(grad_resid)
-    grad_b_out = jnp.sum(grad_branch.astype(jnp.float32), axis=0)
-    grad_w_out = left_product(mixed_heads, grad_branch)
-    grad_mixed = to_bf(right_product(grad_branch, w_out))
-    grad_queries, grad_keys, grad_values = lax.map(
-        page_backward,
-        (
-            split_pages(queries, page_count),
-            split_pages(keys_all, page_count),
-            split_pages(values_all, page_count),
-            lengths,
-            log_total,
-            split_pages(grad_mixed, page_count),
-        ),
-    )
-    grad_queries = grad_queries.reshape(row_count, -1) * HEAD_DIM ** (-0.5)
-    grad_keys = grad_keys.reshape(row_count, -1)
-    grad_values = grad_values.reshape(row_count, -1)
-    grad_w_query = left_product(inputs, grad_queries)
-    grad_b_query = jnp.sum(grad_queries.astype(jnp.float32), axis=0)
-    grad_w_key = left_product(inputs, grad_keys)
-    grad_w_value = left_product(inputs, grad_values)
-    grad_b_value = jnp.sum(grad_values.astype(jnp.float32), axis=0)
-    input_terms = (
-        right_product(grad_queries, w_query)
-        + right_product(grad_keys, w_key)
-        + right_product(grad_values, w_value)
-    )
-    grad_inputs = grad_resid + lax.psum(input_terms, "tensor")
-    grad_grid = grad_inputs.reshape(page_count, page_rows, model_width)
-    grad_tokens = jnp.where(replaced, 0.0, grad_grid).reshape(row_count, model_width)
-    place_table = product(
-        hit_table[0].astype(jnp.bfloat16), pick_table[0].astype(jnp.bfloat16)
-    )
-    place_table = to_bf(place_table)
+    grad_b_out = jnp.sum(grad_branch.astype(F32), axis=0)
+    grad_w_out = left_product(fw["mixed"], grad_branch)
+    key_bias = jnp.where(jnp.arange(row_count) < lengths[0], 0.0, mask_fill).astype(F32)
+
+    def attend_back(first, w_o):
+        queries, keys_all, values_all = (fw[n][first : first + heads] for n in ("q", "k", "v"))
+        grad_mixed = to_bf(right_product(grad_branch, w_o)).reshape(row_count, heads, HEAD_DIM)
+        grad_mixed = grad_mixed.transpose(1, 0, 2)
+        scores = jnp.einsum("hke,hqe->hkq", keys_all, queries, preferred_element_type=F32)
+        probs = jnp.exp(scores + key_bias[None, :, None] - fw["lse"][first : first + heads])
+        grad_probs = jnp.einsum("hke,hqe->hkq", values_all, grad_mixed, preferred_element_type=F32)
+        grad_scores = to_bf(
+            probs * (grad_probs - jnp.sum(probs * grad_probs, axis=1, keepdims=True))
+        )
+        grad_queries = to_bf(
+            jnp.einsum("hkq,hke->qhe", grad_scores, keys_all, preferred_element_type=F32)
+        )
+        grad_keys = to_bf(
+            jnp.einsum("hkq,hqe->khe", grad_scores, queries, preferred_element_type=F32)
+        )
+        grad_values = to_bf(
+            jnp.einsum("hkq,hqe->khe", to_bf(probs), grad_mixed, preferred_element_type=F32)
+        )
+        return (
+            grad_queries.reshape(row_count, -1) * HEAD_DIM ** (-0.5),
+            grad_keys.reshape(row_count, -1),
+            grad_values.reshape(row_count, -1),
+        )
+
+    gq, gk, gv = attend_back(0, w_out)
+    grad_w_query = left_product(inputs, gq)
+    grad_w_key = left_product(inputs, gk)
+    grad_w_value = left_product(inputs, gv)
+    grad_b_query = jnp.sum(gq.astype(F32), axis=0)
+    grad_b_value = jnp.sum(gv.astype(F32), axis=0)
+    oq, ok, ov = attend_back(heads, fw["wo"])
+    own = right_product(gq, w_query) + right_product(gk, w_key) + right_product(gv, w_value)
+    other = right_product(oq, fw["wq"]) + right_product(ok, fw["wk"]) + right_product(ov, fw["wv"])
+    grad_inputs = grad_resid + (own + other)
+    replaced = jnp.sum(place_table.astype(F32), axis=1, keepdims=True) > 0.5
+    grad_tokens = jnp.where(replaced, 0.0, grad_inputs)
     tensor = lax.axis_index("tensor")
     half = model_width // 2
 

time: 497 us -> 437 us (0.88); the launches traced: 496 us -> 430 us
  waiting for transfers between devices: 192 us -> 0.01 us
  Pallas kernels: 155 us -> 262 us
  matrix products: 55 us -> 76.7 us
  local copies, waits for them, and re-layouts: 45.1 us -> 62.3 us
  between operations: 15.2 us -> 1.92 us
  other arithmetic: 33.3 us -> 27.1 us
    psum x4 -> x0, waiting for transfers between devices: 192 us -> none  [the longest x1 54.2 us: forward(): branch = lax.psum(product(mixed_heads, w_out), 'tensor') + b_out]
    pallas_call x0 -> x1, Pallas kernels: none -> 103 us  [call(): pl.pallas_call(kern, out_shape=tuple(outs.values()), in_specs=specs, out_...]
    dot_general x6 -> x11, matrix products: 10.1 us -> 34.1 us  [right_product(): lax.dot_general(left, right, (((1,), (1,)), ((), ())), preferred_element_...]
    convert_element_type x0 -> x3, local copies, waits for them, and re-layouts: none -> 10.7 us  [the longest x2 7.14 us: local(): pre_own = to_bf(right_product(grad_down, w_down) * slope_own)]
    reduce_sum x9 -> x2, other arithmetic: 11.6 us -> 2.5 us  [the longest x1 2.35 us: local(): grad_b_out = jnp.sum(grad_branch.astype(F32), axis=0)]
    dot_general x14 -> x10, matrix products: 32.7 us -> 25.5 us  [the longest x2 8.77 us: attend_back(): jnp.einsum('hke,hqe->hkq', keys_all, queries, preferred_element_type=F32)]
    unnamed x88 -> x80, local copies, waits for them, and re-layouts: 10.2 us -> 9.83 us
  transfers between devices with their start and end apart: 5 -> 1, of which waited for: 4 -> 0; matrix products, arithmetic and copies ran while one was open for 6% -> 6% of each run, Pallas kernels for 0% -> 0%
where the time goes in v2:
time: 437 us; the launch traced here: 430 us
  Pallas kernels  262 us (60%)
  matrix products  76.7 us (18%)
  local copies, waits for them, and re-layouts  62.3 us (14%)
  other arithmetic  27.1 us (6%)
    pallas_call x1, Pallas kernels, comm_only(): pl.pallas_call(kern, out_shape=jax.ShapeDtypeStruct((n, 8, e, w), F32), i...  159 us
    pallas_call x1, Pallas kernels, call(): pl.pallas_call(kern, out_shape=tuple(outs.values()), in_specs=specs, out_...  103 us
    dot_general x11, matrix products, right_product(): lax.dot_general(left, right, (((1,), (1,)), ((), ())), preferred_element_...  34.1 us
    dot_general x8, matrix products, left_product(): lax.dot_general(left, right, (((0,), (0,)), ((), ())), preferred_element_...  17 us
    slice x3, local copies, waits for them, and re-layouts, take(): return summed[at - count:at]  12.8 us
    pad x1, local copies, waits for them, and re-layouts, local(): stack = jnp.pad(stack, ((0, chunks * 8 * eighth - rows), (0, 0)))  11.3 us
    unnamed x80, local copies, waits for them, and re-layouts  9.83 us
    dot_general x2, matrix products, attend_back(): jnp.einsum('hke,hqe->hkq', keys_all, queries, preferred_element_type=F32)  8.77 us
  transfers between devices with their start and end apart: 1, of which 0 were waited for; matrix products, arithmetic and copies ran while one was open for 6% of the time, Pallas kernels for 0%

profile of v2, /device:TPU:0, one launch (start us, length us, event | category | flops | bytes accessed | tf_op | source)
XLA Modules:
  0.0 429.6 jit_solution(12246098654735069462)
XLA Ops:
  8.1 103.0 %forward_gather.1 = (bf16[512,768]{1,0:T(8,128)(2,1)}, bf16[768,384]{1,0:T(8,128)(2,1)}, bf16[768,384]{1,0:T(8,128)(2,1)}, bf16[768,384]{1,0:T(8,128)(2,1)}, bf1...) custom-call(s32[1]{0:T(128)} %copy.95.refs_0_, ...), custom_call_target="tpu_custom_call" | custom-call | tf_op jit(solution)/shard_map/forward_gather/pallas_call | solution.py:270
  111.2 5.2 %fusion.23 = f32[6,512,512]{2,1,0:T(8,128)} fusion(bf16[12,512,64]{2,1,0:T(8,128)(2,1)} %get-tuple-element.49, bf16[12,512,64]{2,1,0:T(8,128)(2,1)} %get-tuple-element.50), kind=kOutput, calls=%fused_computation.65 | convolution fusion | flops 201326592 | bytes 8650752 | tf_op jit(solution)/shard_map/hke,hqe->hkq/dot_general | solution.py:651
  116.3 3.6 fusion.21
  119.9 3.3 convert_bitcast_fusion
  123.3 3.5 copy.53
  126.8 3.6 copy.54
  130.4 4.2 convert_reduce_fusion
  134.6 2.6 fusion.49
  137.2 3.5 copy.55
  140.7 9.1 %multiply_reduce_fusion.2 = (f32[768]{0:T(1024)S(1)}, f32[512]{0:T(512)S(1)}, f32[512]{0:T(512)S(1)}, f32[768]{0:T(1024)S(1)}, f32[512,768]{1,0:T(8,128)}) fusion(f32[512,768]{1,0:T(8,128)} %get-tuple-element.48, f32[768]{0:T(1024)S(1)} %convert_element_type.130, f32[512,768]{1,0:T(8,128)} %get-tuple-element.43, f32[512,768]{1,0:T(8,128)} %fusion.49, ...), kind=kOutput, calls=%fused_computation.38 | convolution fusion | flops 2421028352 | bytes 14955520 | tf_op jit(solution)/shard_map/dot_general | solution.py:35
  150.0 2.4 convert_reduce_fusion.1
  158.1 5.0 %multiply_reduce_fusion.1 = (f32[6,512]{1,0:T(8,128)S(1)}, f32[6,512]{1,0:T(8,128)S(1)}, f32[6,512,512]{2,1,0:T(8,128)}) fusion(f32[6,512,512]{2,1,0:T(8,128)S(1)} %bitcast.101, f32[6,512]{1,0:T(8,128)S(1)} %get-tuple-element.110, f32[512]{0:T(512)S(1)} %fusion.37, f32[6,512,512]{2,1,0:T(8,128)S(1)} %fusion.59, f32[6,512]{1,0:T(8,128)S(1)} %get-tuple-element.109, ...), kind=kOutput, calls=%fused_computation.4 | convolution fusion | flops 213903360 | bytes 26396672 | tf_op jit(solution)/shard_map/hke,hqe->hkq/dot_general | solution.py:653
  163.1 8.0 %multiply_convert_fusion.1 = (bf16[6,512,512]{2,1,0:T(8,128)(2,1)}, bf16[6,512,512]{2,1,0:T(8,128)(2,1)}) fusion(f32[6,512,512]{2,1,0:T(8,128)} %get-tuple-element.98, f32[6,512,512]{2,1,0:T(8,128)S(1)} %bitcast.101, f32[6,512]{1,0:T(8,128)S(1)} %get-tuple-element.72, f32[6,512]{1,0:T(8,128)S(1)} %get-tuple-element.110, f32[512]{0:T(512)S(1)} %fusion.37, ...), kind=kLoop, calls=%fused_computation.3 | loop fusion | flops 15728640 | bytes 31508480 | tf_op jit(solution)/shard_map/convert_element_type | solution.py:21
  171.2 3.3 convolution_convert_fusion.2
  177.7 1.8 convolution_convert_fusion
  180.9 2.0 fusion.15
  184.5 1.7 fusion.51
  186.2 1.8 fusion.50
  191.3 1.8 fusion.52
  194.9 3.1 fusion.54
  198.0 2.9 fusion.53
  200.9 5.9 %broadcast_select_fusion = (f32[512,768]{1,0:T(8,128)}, f32[512,768]{1,0:T(8,128)S(1)}) fusion(pred[512]{0:T(512)(128)(4,1)S(1)} %broadcast_compare_fusion, bf16[512,384]{0,1:T(8,128)(2,1)} %bitcast.128, bf16[768,384]{1,0:T(8,128)(2,1)} %get-tuple-element.56, f32[512,768]{1,0:T(8,128)} %fusion.53, f32[512,768]{1,0:T(8,128)} %fusion.54, ...), kind=kOutput, calls=%fused_computation.67 | convolution fusion | flops 306708480 | bytes 15148544 | tf_op jit(solution)/shard_map/dot_general | solution.py:35
  208.3 4.9 %fusion.55 = f32[768,1536]{1,0:T(8,128)} fusion(bf16[512,768]{1,0:T(8,128)(2,1)} %get-tuple-element.58, bf16[512,1536]{1,0:T(8,128)(2,1)S(1)} %copy-done.6), kind=kOutput, calls=%fused_computation.113 | convolution fusion | flops 1207959552 | bytes 7077888 | tf_op jit(solution)/shard_map/dot_general | solution.py:29
  213.1 2.7 copy.66
  215.8 5.1 %convolution_dynamic-update-slice_fusion = f32[4742,768]{1,0:T(8,128)} fusion(bf16[512,1536]{0,1:T(8,128)(2,1)} %bitcast.126, bf16[512,768]{1,0:T(8,128)(2,1)S(1)} %copy-done.21), kind=kOutput, calls=%fused_computation.7 | convolution fusion | flops 1207959552 | bytes 7077888 | tf_op jit(solution)/shard_map/dot_general | solution.py:29
  222.5 1.6 slice_dynamic-update-slice_fusion
  230.0 11.3 %pad.4 = f32[4800,768]{1,0:T(8,128)} pad(f32[4742,768]{1,0:T(8,128)} %constant_dynamic-update-slice_fusion, f32[]{:T(128)} %constant.9.clone.1), padding=0_58x0_0 | pad | bytes 29313028 | tf_op jit(solution)/shard_map/jit(_pad)/pad | solution.py:725
  241.3 158.6 %sum_dp.1 = f32[25,8,24,768]{3,2,1,0:T(8,128)} custom-call(f32[25,8,24,768]{3,2,1,0:T(8,128)} %bitcast.104), custom_call_target="tpu_custom_call" | custom-call | tf_op jit(solution)/shard_map/sum_dp/pallas_call | solution.py:206
  401.8 5.1 %fusion.42 = (f32[4,8,24,768]{3,2,1,0:T(8,128)S(1)}, f32[4,8,24,768]{3,2,1,0:T(8,128)}, f32[4,8,24,768]{3,2,1,0:T(8,128)S(1)}) fusion(f32[25,8,24,768]{3,2,1,0:T(8,128)} %sum_dp.1), kind=kLoop, calls=%fused_computation.100 | loop fusion | bytes 14155776 | tf_op jit(solution)/shard_map/slice | solution.py:737
  406.9 2.8 fusion.43
  415.1 4.9 %slice.186 = f32[8,8,24,768]{3,2,1,0:T(8,128)} slice(f32[25,8,24,768]{3,2,1,0:T(8,128)} %sum_dp.1), slice={[0:8], [0:8], [0:24], [0:768]} | slice | bytes 9437184 | tf_op jit(solution)/shard_map/slice | solution.py:737
  421.3 4.4 %pad_maximum_fusion = f32[768,1536]{1,0:T(8,128)} fusion(f32[768,768]{1,0:T(8,128)} %bitcast.113, f32[768,768]{1,0:T(8,128)S(1)} %bitcast.112), kind=kLoop, calls=%fused_computation.6 | loop fusion | flops 1179648 | bytes 9437184 | tf_op jit(solution)/shard_map/concatenate | solution.py:740
  (143 shorter events, 44.9 us)
Async XLA Ops:
  111.1 5.2 %copy-start = (bf16[12,512,64]{2,1,0:T(8,128)(2,1)S(1)}, bf16[12,512,64]{2,1,0:T(8,128)(2,1)}, u32[]{:S(2)}) copy-start(bf16[12,512,64]{2,1,0:T(8,128)(2,1)} %get-tuple-element.49) | copy-start | bytes 2359300
  111.1 5.2 %copy-start.29 = (bf16[12,512,64]{2,1,0:T(8,128)(2,1)S(1)}, bf16[12,512,64]{2,1,0:T(8,128)(2,1)}, u32[]{:S(2)}) copy-start(bf16[12,512,64]{2,1,0:T(8,128)(2,1)} %get-tuple-element.50) | copy-start | bytes 2359300
  116.3 3.6 copy-start.12
  126.8 3.6 copy-start.20
  130.4 4.2 copy-start.18
  134.6 2.6 copy-start.5
  140.7 9.1 %copy-start.27 = (f32[512,1]{1,0:T(8,128)S(1)}, f32[512,1]{1,0:T(8,128)}, u32[]{:S(2)}) copy-start(f32[512,1]{1,0:T(8,128)} %get-tuple-element.42) | copy-start | bytes 6148
  149.8 2.6 copy-start.23
  150.0 2.9 copy-start.31
  152.4 3.1 slice-start.2
  152.9 3.8 slice-start
  154.1 3.4 slice-start.1
  154.1 4.0 slice-start.3
  171.2 3.4 copy-start.1
  175.3 1.9 copy-start.2
  175.3 2.4 copy-start.30
  180.9 3.6 copy-start.15
  183.0 3.3 copy-start.16
  184.5 3.5 copy-start.3
  188.0 3.3 copy-start.17
  191.3 3.4 copy-start.19
  194.9 6.0 %copy-start.7 = (f32[512,768]{1,0:T(8,128)S(1)}, f32[512,768]{1,0:T(8,128)}, u32[]{:S(2)}) copy-start(f32[512,768]{1,0:T(8,128)} %get-tuple-element.48) | copy-start | bytes 4718596
  194.9 6.0 %copy-start.8 = (f32[512,768]{1,0:T(8,128)S(1)}, f32[512,768]{1,0:T(8,128)}, u32[]{:S(2)}) copy-start(f32[512,768]{1,0:T(8,128)} %get-tuple-element.97) | copy-start | bytes 4718596
  213.1 2.7 copy-start.21
  213.1 7.8 %slice-start.4 = ((s8[4718592]{0:T(1024)(128)(4,1)}), s8[524288]{0:T(1024)(128)(4,1)S(1)}, s32[]{:S(2)}) async-start(s8[4718592]{0:T(1024)(128)(4,1)} %bitcast.108), calls=%async_computation.4 | async-start | bytes 1048576
  215.8 5.1 %slice-start.5 = ((s8[4718592]{0:T(1024)(128)(4,1)}), s8[4194304]{0:T(1024)(128)(4,1)S(1)}, s32[]{:S(2)}) async-start(s8[4718592]{0:T(1024)(128)(4,1)} %bitcast.108), calls=%async_computation.5 | async-start | bytes 8388608
  222.5 2.3 copy-start.14
  222.5 2.4 copy-start.24
  224.2 2.3 copy-start.10
  224.2 2.3 copy-start.11
  401.7 24.0 %collective-permute-start = (f32[264,384]{1,0:T(8,128)}, f32[264,384]{1,0:T(8,128)}, u32[]{:S(2)}, u32[]{:S(2)}) collective-permute-start(f32[264,384]{1,0:T(8,128)} %slice.162), channel_id=1, source_target_pairs={{0,1},{1,0},{2,3},{3,2},{4,5},{5,4},{6,7},{7,6},{8,9},{9,8},{10,11... | collective-permute-start | bytes 1216520 | tf_op jit(solution)/shard_map/ppermute | solution.py:749
  425.7 2.8 copy-start.22
  (7 other events, 10.0 us)
